TPU v7x, 32 devices: a whole 2x2x4 slice. The times are simulated.
32 devices in a mesh: seq: 8 (over y, x, core), zero: 4 (over z).
Axes of the slice: x: 2, y: 2, z: 4, core: 2. Of those that a mesh axis runs over, the one named last changes fastest.
Arguments:
- tokens: bfloat16 [4096, 1024], P(('seq', 'zero')), may hold values from -18 to 18
- projection: bfloat16 [1024, 3072], P('zero'), may hold values from -0.1875 to 0.1875
- pattern: int32 [32, 8], replicated, may hold values from 0 to 31, as said below
- upstream: bfloat16 [4096, 1024], P(('seq', 'zero')), may hold values from -6 to 6
Outputs:
- attended: bfloat16 [4096, 1024], P(('seq', 'zero'))
- token_gradient: bfloat16 [4096, 1024], P(('seq', 'zero'))
- weight_gradient: float32 [1024, 3072], P('zero')
Inputs may be any that keep to these rules, and one draw needn't show every extreme that they name: `pattern`: each row names 8 different key blocks, block 0 and the row's own block among them.
All inputs are finite; a program needn't handle non-finite values.
Results may differ from a plain program's by a relative error of at most 0.01.
The roundings to bfloat16 on the way count: a program that leaves them out, or rounds other values in their place, can miss the bound.
Values may be sent and summed in bfloat16 or wider, within the bound.
A program may use at most 128 MiB of HBM per device.

v0:
```python
import jax
import jax.numpy as jnp
from jax import lax
from jax.sharding import PartitionSpec as P

HEADS = 16
HEAD = 64
BLOCK = 128
NBK = 8


def on_device(tokens, projection, pattern, upstream):
    seq_count = lax.axis_size("seq")
    zero_count = lax.axis_size("zero")
    zero_index = lax.axis_index("zero")
    tok_rows = tokens.shape[0]
    model_width = tokens.shape[1]
    heads_here = HEADS // seq_count
    head_cols = heads_here * HEAD
    per_shard = tok_rows // BLOCK
    local_blocks = seq_count * per_shard
    group_size = 4
    step_count = local_blocks // group_size
    score_scale = HEAD ** (-0.5)
    weights = lax.all_gather(projection, "zero", axis=0, tiled=True)
    projected = jnp.dot(tokens, weights, preferred_element_type=jnp.float32).astype(jnp.bfloat16)
    projected = projected.reshape(tok_rows, 3, seq_count, head_cols)
    by_head = lax.all_to_all(projected, "seq", split_axis=2, concat_axis=0, tiled=True)
    by_head = by_head.reshape(local_blocks * BLOCK, 3, head_cols)
    key_all, value_all = (
        lax.all_gather(by_head[:, 1], "zero", axis=0, tiled=True),
        lax.all_gather(by_head[:, 2], "zero", axis=0, tiled=True),
    )
    key_all = key_all.reshape(zero_count * local_blocks, BLOCK, heads_here, HEAD)
    value_all = value_all.reshape(zero_count * local_blocks, BLOCK, heads_here, HEAD)
    queries = by_head[:, 0].reshape(step_count, group_size, BLOCK, heads_here, HEAD)
    incoming = lax.all_to_all(
        upstream.reshape(tok_rows, seq_count, head_cols),
        "seq",
        split_axis=1,
        concat_axis=0,
        tiled=True,
    )
    incoming = incoming.reshape(step_count, group_size, BLOCK, heads_here, HEAD)
    local_ids = jnp.arange(local_blocks, dtype=jnp.int32)
    row_ids = (local_ids // per_shard * zero_count + zero_index) * per_shard + local_ids % per_shard
    row_lists = pattern[row_ids]
    shard_ids = row_lists // per_shard
    key_slots = (
        shard_ids % zero_count * local_blocks
        + shard_ids // zero_count * per_shard
        + row_lists % per_shard
    )
    key_slots = key_slots.reshape(step_count, group_size, NBK)

    def attend(carried, inputs):
        key_grad, value_grad = carried
        query_block, up_block, slot_block = inputs
        key_chosen = key_all[slot_block].reshape(group_size, NBK * BLOCK, heads_here, HEAD)
        value_chosen = value_all[slot_block].reshape(group_size, NBK * BLOCK, heads_here, HEAD)
        scores = (
            jnp.einsum(
                "rqhe,rkhe->rhqk", query_block, key_chosen, preferred_element_type=jnp.float32
            )
            * score_scale
        )
        row_max = jnp.max(scores, axis=-1, keepdims=True)
        exponent = jnp.exp(scores - row_max)
        prob_full = exponent / jnp.sum(exponent, axis=-1, keepdims=True)
        prob_low = prob_full.astype(jnp.bfloat16)
        out_block = jnp.einsum(
            "rhqk,rkhe->rqhe", prob_low, value_chosen, preferred_element_type=jnp.float32
        ).astype(jnp.bfloat16)
        prob_grad = jnp.einsum(
            "rqhe,rkhe->rhqk", up_block, value_chosen, preferred_element_type=jnp.float32
        )
        row_delta = jnp.sum(prob_full * prob_grad, axis=-1, keepdims=True)
        score_grad = (prob_full * (prob_grad - row_delta) * score_scale).astype(jnp.bfloat16)
        query_grad = jnp.einsum(
            "rhqk,rkhe->rqhe", score_grad, key_chosen, preferred_element_type=jnp.float32
        ).astype(jnp.bfloat16)
        key_terms = jnp.einsum(
            "rhqk,rqhe->rkhe", score_grad, query_block, preferred_element_type=jnp.float32
        )
        value_terms = jnp.einsum(
            "rhqk,rqhe->rkhe", prob_low, up_block, preferred_element_type=jnp.float32
        )
        key_grad = key_grad.at[slot_block].add(
            key_terms.reshape(group_size, NBK, BLOCK, heads_here, HEAD)
        )
        value_grad = value_grad.at[slot_block].add(
            value_terms.reshape(group_size, NBK, BLOCK, heads_here, HEAD)
        )
        return ((key_grad, value_grad), (out_block, query_grad))

    zero_start = jnp.zeros((zero_count * local_blocks, BLOCK, heads_here, HEAD), jnp.float32)
    (key_grad, value_grad), (out_blocks, query_grads) = lax.scan(
        attend, (zero_start, zero_start), (queries, incoming, key_slots)
    )
    attended = lax.all_to_all(
        out_blocks.reshape(local_blocks * BLOCK, 1, head_cols),
        "seq",
        split_axis=0,
        concat_axis=1,
        tiled=True,
    )
    attended = attended.reshape(tok_rows, seq_count * head_cols)
    key_sum, value_sum = (
        lax.psum_scatter(
            key_grad.astype(jnp.bfloat16), "zero", scatter_dimension=0, tiled=True
        ).astype(jnp.float32),
        lax.psum_scatter(
            value_grad.astype(jnp.bfloat16), "zero", scatter_dimension=0, tiled=True
        ).astype(jnp.float32),
    )
    local_grads = jnp.stack(
        [
            query_grads.reshape(-1, head_cols),
            key_sum.astype(jnp.bfloat16).reshape(-1, head_cols),
            value_sum.astype(jnp.bfloat16).reshape(-1, head_cols),
        ],
        axis=1,
    )
    local_grads = local_grads.reshape(local_blocks * BLOCK, 3, 1, head_cols)
    token_grads = lax.all_to_all(local_grads, "seq", split_axis=0, concat_axis=2, tiled=True)
    flat_grads = token_grads.reshape(tok_rows, 3 * seq_count * head_cols)
    token_gradient = jnp.einsum(
        "tc,dc->td", flat_grads, weights, preferred_element_type=jnp.float32
    ).astype(jnp.bfloat16)
    shard_rows = model_width // zero_count
    grouped_tokens = lax.all_gather(tokens, "seq", axis=0, tiled=True)
    head_flat = local_grads.reshape(local_blocks * BLOCK, 3 * head_cols)
    own_rows = lax.psum_scatter(
        jnp.einsum("td,tc->dc", grouped_tokens, head_flat, preferred_element_type=jnp.float32),
        "zero",
        scatter_dimension=0,
        tiled=True,
    )
    own_rows = own_rows.reshape(shard_rows, 3, 1, head_cols)
    weight_gradient = lax.all_gather(own_rows, "seq", axis=2, tiled=True).reshape(
        shard_rows, 3 * seq_count * head_cols
    )
    return (attended, token_gradient, weight_gradient)


def solution(mesh):
    return jax.shard_map(
        on_device,
        mesh=mesh,
        in_specs=(P(("seq", "zero"), None), P("zero", None), P(), P(("seq", "zero"), None)),
        out_specs=(P(("seq", "zero"), None), P(("seq", "zero"), None), P("zero", None)),
        check_vma=False,
    )
```

profile of v0, /device:TPU:11, one launch (start us, length us, event | category | flops | bytes accessed | tf_op | source)
XLA Modules:
  0.0 534.2 jit_solution(16270815817319712212)
XLA Ops:
  8.8 115.4 %all-gather.8.cloned.1.call-done = bf16[1024,3072]{1,0:T(8,128)(2,1)} async-done(((bf16[256,3072]{1,0:T(8,128)(2,1)}), bf16[1024,3072]{1,0:T(8,128)(2,1)}) %all-gather.8.cloned.1.call-update) | async-done | bytes 6291472 | tf_op jit(solution)/shard_map/all_gather | solution.py:25
  128.4 15.2 %all_to_all.60 = bf16[128,3,8,128]{3,0,1,2:T(8,128)(2,1)S(1)} all-to-all(bf16[128,3,8,128]{3,0,1,2:T(8,128)(2,1)S(1)} %copy.100), channel_id=1, replica_groups=mesh['seq'=8,'zero'=4] {'seq'}, dimensions={2} | all-to-all | bytes 1572864 | tf_op jit(solution)/shard_map/all_to_all | solution.py:28
  153.1 19.3 %all-gather.14.cloned.1.call-done = bf16[4096,1,128]{2,0,1:T(8,128)(2,1)} async-done(((bf16[1024,1,128]{2,0,1:T(8,128)(2,1)}), bf16[4096,1,128]{2,0,1:T(8,128)(2,1)}) %all-gather.14.cloned.1.call-update) | async-done | bytes 1048592 | tf_op jit(solution)/shard_map/all_gather | solution.py:31
  177.4 24.6 %all-gather.16.cloned.1.call-done = bf16[4096,1,128]{2,0,1:T(8,128)(2,1)} async-done(((bf16[1024,1,128]{2,0,1:T(8,128)(2,1)}), bf16[4096,1,128]{2,0,1:T(8,128)(2,1)}) %all-gather.16.cloned.1.call-update) | async-done | bytes 1048592 | tf_op jit(solution)/shard_map/all_gather | solution.py:32
  210.1 164.7 %while.16 = (s32[]{:T(128)}, f32[32,128,2,64]{1,3,2,0:T(8,128)}, f32[32,128,2,64]{1,3,2,0:T(8,128)}, bf16[2,4,128,2,64]{2,4,3,1,0:T(8,128)(2,1)}, bf16[2,4,128,2...) while((s32[]{:T(128)}, f32[32,128,2,64]{1,3,2,0:T(8,128)}, ...), condition=%wide.region_6.7_spmd, body=%wide.region_0.6_spmd.sunk | while | flops 828512384 | bytes 108034936 | solution.py:97
  210.2 7.0 %gather_fusion.1 = bf16[32,128,2,64]{3,2,1,0:T(2,128)(2,1)S(1)} fusion(bf16[32,128,2,64]{3,2,1,0:T(2,128)(2,1)} %get-tuple-element.230, s32[1024]{0:T(1024)S(1)} %pad_clamp_fusion.3), kind=kCustom, calls=%fused_computation.clone.1 | custom fusion | bytes 2097280 | tf_op jit(solution)/shard_map/while/body/eval_jaxpr/gather | solution.py:59
  223.3 7.0 %gather_fusion = bf16[32,128,2,64]{3,2,1,0:T(2,128)(2,1)S(1)} fusion(bf16[32,128,2,64]{3,2,1,0:T(2,128)(2,1)} %get-tuple-element.232, s32[1024]{0:T(1024)S(1)} %pad_clamp_fusion.3), kind=kCustom, calls=%fused_computation.1.clone.1 | custom fusion | bytes 2097280 | tf_op jit(solution)/shard_map/while/body/eval_jaxpr/gather | solution.py:60
  234.6 11.5 %fusion.118 = bf16[1,4,128,2,64]{2,4,3,1,0:T(8,128)(2,1)S(1)} fusion(bf16[4,1024,2,64]{1,3,2,0:T(8,128)(2,1)S(1)} %copy-done.2, f32[4,2,128,1024]{3,2,1,0:T(8,128)} %fusion.114, f32[4,2,128,1024]{3,2,1,0:T(8,128)} %get-tuple-element.199, f32[4,2,128]{2,1,0:T(2,128)S(1)} %get-tuple-element.200), kind=kOutput, calls=%fused_computation.25.clone.1 | convolution fusion | flops 141625344 | bytes 9572352 | tf_op jit(solution)/shard_map/while/body/eval_jaxpr/rhqk,rkhe->rqhe/dot_general | solution.py:79
  255.7 6.2 %scatter_fusion.1 = f32[32,128,2,64]{1,3,2,0:T(8,128)} fusion(f32[32,128,2,64]{1,3,2,0:T(8,128)} %get-tuple-element.214, s32[32]{0:T(128)S(1)} %reshape.199, f32[32,128,2,64]{1,3,2,0:T(8,128)S(1)} %copy.147), kind=kCustom, calls=%fused_computation.4.clone.1 | custom fusion | flops 524288 | bytes 6291584 | tf_op jit(solution)/shard_map/while/body/eval_jaxpr/scatter-add | solution.py:91
  261.9 13.1 %fusion.116 = f32[4,1024,2,64]{1,3,2,0:T(8,128)} fusion(f32[4,2,128,1024]{3,2,1,0:T(8,128)} %fusion.114, bf16[2,4,128,2,64]{2,4,3,1,0:T(8,128)(2,1)} %get-tuple-element.229, s32[]{:T(128)} %get-tuple-element.212, f32[4,2,128,1024]{3,2,1,0:T(8,128)} %get-tuple-element.199, f32[4,2,128]{2,1,0:T(2,128)S(1)} %get-tuple-element.200), kind=kOutput, calls=%fused_computation.19.clone.1 | convolution fusion | flops 141559808 | bytes 19014144 | tf_op jit(solution)/shard_map/while/body/eval_jaxpr/rhqk,rqhe->rkhe/dot_general | solution.py:82
  282.6 6.1 %scatter_fusion = f32[32,128,2,64]{1,3,2,0:T(8,128)} fusion(f32[32,128,2,64]{1,3,2,0:T(8,128)} %get-tuple-element.213, s32[32]{0:T(128)S(1)} %reshape.199, f32[32,128,2,64]{1,3,2,0:T(8,128)S(1)} %copy.145), kind=kCustom, calls=%fused_computation.3.clone.1 | custom fusion | flops 524288 | bytes 6291584 | tf_op jit(solution)/shard_map/while/body/eval_jaxpr/scatter-add | solution.py:88
  292.5 7.0 %gather_fusion.1 = bf16[32,128,2,64]{3,2,1,0:T(2,128)(2,1)S(1)} fusion(bf16[32,128,2,64]{3,2,1,0:T(2,128)(2,1)} %get-tuple-element.230, s32[1024]{0:T(1024)S(1)} %pad_clamp_fusion.3), kind=kCustom, calls=%fused_computation.clone.1 | custom fusion | bytes 2097280 | tf_op jit(solution)/shard_map/while/body/eval_jaxpr/gather | solution.py:59
  305.6 7.0 %gather_fusion = bf16[32,128,2,64]{3,2,1,0:T(2,128)(2,1)S(1)} fusion(bf16[32,128,2,64]{3,2,1,0:T(2,128)(2,1)} %get-tuple-element.232, s32[1024]{0:T(1024)S(1)} %pad_clamp_fusion.3), kind=kCustom, calls=%fused_computation.1.clone.1 | custom fusion | bytes 2097280 | tf_op jit(solution)/shard_map/while/body/eval_jaxpr/gather | solution.py:60
  316.9 11.5 %fusion.118 = bf16[1,4,128,2,64]{2,4,3,1,0:T(8,128)(2,1)S(1)} fusion(bf16[4,1024,2,64]{1,3,2,0:T(8,128)(2,1)S(1)} %copy-done.2, f32[4,2,128,1024]{3,2,1,0:T(8,128)} %fusion.114, f32[4,2,128,1024]{3,2,1,0:T(8,128)} %get-tuple-element.199, f32[4,2,128]{2,1,0:T(2,128)S(1)} %get-tuple-element.200), kind=kOutput, calls=%fused_computation.25.clone.1 | convolution fusion | flops 141625344 | bytes 9572352 | tf_op jit(solution)/shard_map/while/body/eval_jaxpr/rhqk,rkhe->rqhe/dot_general | solution.py:79
  338.0 6.2 %scatter_fusion.1 = f32[32,128,2,64]{1,3,2,0:T(8,128)} fusion(f32[32,128,2,64]{1,3,2,0:T(8,128)} %get-tuple-element.214, s32[32]{0:T(128)S(1)} %reshape.199, f32[32,128,2,64]{1,3,2,0:T(8,128)S(1)} %copy.147), kind=kCustom, calls=%fused_computation.4.clone.1 | custom fusion | flops 524288 | bytes 6291584 | tf_op jit(solution)/shard_map/while/body/eval_jaxpr/scatter-add | solution.py:91
  344.2 13.1 %fusion.116 = f32[4,1024,2,64]{1,3,2,0:T(8,128)} fusion(f32[4,2,128,1024]{3,2,1,0:T(8,128)} %fusion.114, bf16[2,4,128,2,64]{2,4,3,1,0:T(8,128)(2,1)} %get-tuple-element.229, s32[]{:T(128)} %get-tuple-element.212, f32[4,2,128,1024]{3,2,1,0:T(8,128)} %get-tuple-element.199, f32[4,2,128]{2,1,0:T(2,128)S(1)} %get-tuple-element.200), kind=kOutput, calls=%fused_computation.19.clone.1 | convolution fusion | flops 141559808 | bytes 19014144 | tf_op jit(solution)/shard_map/while/body/eval_jaxpr/rhqk,rqhe->rkhe/dot_general | solution.py:82
  365.0 6.1 %scatter_fusion = f32[32,128,2,64]{1,3,2,0:T(8,128)} fusion(f32[32,128,2,64]{1,3,2,0:T(8,128)} %get-tuple-element.213, s32[32]{0:T(128)S(1)} %reshape.199, f32[32,128,2,64]{1,3,2,0:T(8,128)S(1)} %copy.145), kind=kCustom, calls=%fused_computation.3.clone.1 | custom fusion | flops 524288 | bytes 6291584 | tf_op jit(solution)/shard_map/while/body/eval_jaxpr/scatter-add | solution.py:88
  380.0 22.9 %reduce-scatter.4.cloned.1.call-done = bf16[8,128,2,64]{1,3,2,0:T(8,128)(2,1)} async-done(((bf16[32,128,2,64]{1,3,2,0:T(8,128)(2,1)}), bf16[8,128,2,64]{1,3,2,0:T(8,128)(2,1)}) %reduce-scatter.4.cloned.1.call-update) | async-done | bytes 262160 | tf_op jit(solution)/shard_map/reduce_scatter | solution.py:109
  404.2 27.4 %reduce-scatter.6.cloned.1.call-done = bf16[8,128,2,64]{1,3,2,0:T(8,128)(2,1)} async-done(((bf16[32,128,2,64]{1,3,2,0:T(8,128)(2,1)}), bf16[8,128,2,64]{1,3,2,0:T(8,128)(2,1)}) %reduce-scatter.6.cloned.1.call-update) | async-done | bytes 262160 | tf_op jit(solution)/shard_map/reduce_scatter | solution.py:112
  436.7 34.2 %reduce-scatter.8.cloned.1.call-done = f32[256,384]{0,1:T(8,128)} async-done(((f32[1024,384]{0,1:T(8,128)}), f32[256,384]{0,1:T(8,128)}) %reduce-scatter.8.cloned.1.call-update) | async-done | bytes 393232 | tf_op jit(solution)/shard_map/reduce_scatter | solution.py:133
  477.1 5.3 all-to-all-start.2
  488.5 7.2 %all-to-all-start.3 = ((bf16[1024,3,1,128]{3,1,2,0:T(4,128)(2,1)}), bf16[1024,3,1,128]{3,1,2,0:T(4,128)(2,1)S(1)}, u32[]{:S(2)}, u32[]{:S(2)}) async-start(bf16[1024,3,1,128]{3,1,2,0:T(4,128)(2,1)} %copy.115), calls=%async_computation.5 | async-start | bytes 2097152 | tf_op jit(solution)/shard_map/all_to_all | solution.py:125
  497.0 18.7 %all-to-all-done.3 = bf16[1024,3,1,128]{3,1,2,0:T(4,128)(2,1)S(1)} async-done(((bf16[1024,3,1,128]{3,1,2,0:T(4,128)(2,1)}), bf16[1024,3,1,128]{3,1,2,0:T(4,128)(2,1)S(1)}, u32[]{:S(2)}, u32[]{:S(2)}) %all-to-all-start.3) | async-done | bytes 786464 | tf_op jit(solution)/shard_map/all_to_all | solution.py:125
  516.2 5.8 %convolution_convert_fusion.2 = bf16[128,1024]{1,0:T(8,128)(2,1)} fusion(bf16[128,3072]{0,1:T(8,128)(2,1)S(1)} %bitcast.137, bf16[1024,3072]{1,0:T(8,128)(2,1)} %all-gather.8.cloned.1.call-done), kind=kOutput, calls=%fused_computation.57 | convolution fusion | flops 805437440 | bytes 7340032 | tf_op jit(solution)/shard_map/tc,dc->td/dot_general | solution.py:127
  (124 shorter events, 120.3 us)
Async XLA Ops:
  8.0 116.2 %all-gather.8.cloned.1.call-start = ((), (), s32[]{:S(2)}) async-start(), calls=%async_computation.7 | async-start | bytes 7864320 | tf_op jit(solution)/shard_map/all_gather | solution.py:25
  8.7 163.6 %all-gather.14.cloned.1.call-start = ((), (), s32[]{:S(2)}) async-start(), calls=%async_computation.13 | async-start | bytes 1310720 | tf_op jit(solution)/shard_map/all_gather | solution.py:31
  128.1 17.2 %copy-start.4 = (bf16[128,1024]{1,0:T(8,128)(2,1)S(1)}, bf16[128,1024]{1,0:T(8,128)(2,1)}, u32[]{:S(2)}) copy-start(bf16[128,1024]{1,0:T(8,128)(2,1)} %param.9) | copy-start | bytes 786436
  128.2 22.9 %copy-start.8 = (s32[32,8]{0,1:T(8,128)S(1)}, s32[32,8]{0,1:T(8,128)}, u32[]{:S(2)}) copy-start(s32[32,8]{0,1:T(8,128)} %param.8) | copy-start | bytes 3076
  144.6 57.4 %all-gather.16.cloned.1.call-start = ((), (), s32[]{:S(2)}) async-start(), calls=%async_computation.14 | async-start | bytes 1310720 | tf_op jit(solution)/shard_map/all_gather | solution.py:32
  146.1 60.8 %all-to-all-start.1 = ((bf16[128,8,128]{0,2,1:T(8,128)(2,1)}), bf16[128,8,128]{0,2,1:T(8,128)(2,1)S(1)}, u32[]{:S(2)}, u32[]{:S(2)}) async-start(bf16[128,8,128]{0,2,1:T(8,128)(2,1)} %bitcast.18), calls=%async_computation.1 | async-start | bytes 524288 | tf_op jit(solution)/shard_map/all_to_all | solution.py:37
  151.1 251.8 %reduce-scatter.4.cloned.1.call-start = ((), (), s32[]{:S(2)}) async-start(), calls=%async_computation.8 | async-start | bytes 1310720 | tf_op jit(solution)/shard_map/reduce_scatter | solution.py:109
  218.7 11.6 %copy-start.1 = (bf16[4,1024,2,64]{1,3,2,0:T(8,128)(2,1)}, bf16[4,1024,2,64]{1,3,2,0:T(8,128)(2,1)S(1)}, u32[]{:S(2)}) copy-start(bf16[4,1024,2,64]{1,3,2,0:T(8,128)(2,1)S(1)} %copy.143) | copy-start | bytes 3145732 | tf_op jit(solution)/shard_map/while
  231.8 2.8 copy-start.2
  234.6 11.5 %copy-start.5 = (bf16[2,4,128,2,64]{2,1,0,4,3:T(4,128)(2,1)S(1)}, bf16[2,4,128,2,64]{2,1,0,4,3:T(4,128)(2,1)}, u32[]{:S(2)}) copy-start(bf16[2,4,128,2,64]{2,1,0,4,3:T(4,128)(2,1)} %get-tuple-element.216) | copy-start | bytes 786436 | tf_op jit(solution)/shard_map/while
  246.3 0.7 copy-start.6
  301.0 11.6 %copy-start.1 = (bf16[4,1024,2,64]{1,3,2,0:T(8,128)(2,1)}, bf16[4,1024,2,64]{1,3,2,0:T(8,128)(2,1)S(1)}, u32[]{:S(2)}) copy-start(bf16[4,1024,2,64]{1,3,2,0:T(8,128)(2,1)S(1)} %copy.143) | copy-start | bytes 3145732 | tf_op jit(solution)/shard_map/while
  314.1 2.8 copy-start.2
  316.9 11.5 %copy-start.5 = (bf16[2,4,128,2,64]{2,1,0,4,3:T(4,128)(2,1)S(1)}, bf16[2,4,128,2,64]{2,1,0,4,3:T(4,128)(2,1)}, u32[]{:S(2)}) copy-start(bf16[2,4,128,2,64]{2,1,0,4,3:T(4,128)(2,1)} %get-tuple-element.216) | copy-start | bytes 786436 | tf_op jit(solution)/shard_map/while
  328.6 0.7 copy-start.6
  374.8 3.1 copy-start
  374.8 4.9 copy-start.7
  377.9 53.7 %reduce-scatter.6.cloned.1.call-start = ((), (), s32[]{:S(2)}) async-start(), calls=%async_computation.9 | async-start | bytes 1310720 | tf_op jit(solution)/shard_map/reduce_scatter | solution.py:112
  379.1 53.8 %all-gather.10.cloned.1.call-start = ((), (), s32[]{:S(2)}) async-start(), calls=%async_computation.10 | async-start | bytes 2359296 | tf_op jit(solution)/shard_map/all_gather | solution.py:131
  379.7 91.2 %reduce-scatter.8.cloned.1.call-start = ((), (), s32[]{:S(2)}) async-start(), calls=%async_computation.11 | async-start | bytes 1966080 | tf_op jit(solution)/shard_map/reduce_scatter | solution.py:133
  432.8 40.0 %copy-start.3 = (bf16[2,4,128,2,64]{2,4,3,1,0:T(8,128)(2,1)S(1)}, bf16[2,4,128,2,64]{2,4,3,1,0:T(8,128)(2,1)}, u32[]{:S(2)}) copy-start(bf16[2,4,128,2,64]{2,4,3,1,0:T(8,128)(2,1)} %get-tuple-element.58) | copy-start | bytes 786436
  436.7 85.3 %all-gather.12.cloned.1.call-start = ((), (), s32[]{:S(2)}) async-start(), calls=%async_computation.12 | async-start | bytes 3538944 | tf_op jit(solution)/shard_map/all_gather | solution.py:140
  477.1 11.4 %all-to-all-start.2 = ((bf16[8,2,8192]{2,1,0:T(2,128)(2,1)}), bf16[8,2,8192]{2,1,0:T(2,128)(2,1)S(1)}, u32[]{:S(2)}, u32[]{:S(2)}) async-start(bf16[8,2,8192]{2,1,0:T(2,128)(2,1)} %reshape.178), calls=%async_computation.2 | async-start | bytes 524288 | tf_op jit(solution)/shard_map/all_to_all | solution.py:100
  488.5 27.2 %all-to-all-start.3 = ((bf16[1024,3,1,128]{3,1,2,0:T(4,128)(2,1)}), bf16[1024,3,1,128]{3,1,2,0:T(4,128)(2,1)S(1)}, u32[]{:S(2)}, u32[]{:S(2)}) async-start(bf16[1024,3,1,128]{3,1,2,0:T(4,128)(2,1)} %copy.115), calls=%async_computation.5 | async-start | bytes 2097152 | tf_op jit(solution)/shard_map/all_to_all | solution.py:125
Sparse Core Ops, SparseCore 0:
  10.4 113.7 all-gather.7
  144.7 27.6 all-gather.13
  174.5 27.4 all-gather.15
  378.0 24.8 reduce-scatter.3
  405.7 25.7 reduce-scatter.5
  436.8 34.0 reduce-scatter.7
Sparse Core Ops, SparseCore 1:
  381.5 27.9 all-gather.9
  472.9 46.8 all-gather.11
where the time goes:
time: 541 us; the launch traced here: 534 us
  waiting for transfers between devices  269 us (50%)
  local copies, waits for them, and re-layouts  94.8 us (18%)
  matrix products  90.2 us (17%)
  other arithmetic  31 us (6%)
  starting transfers between devices  17.8 us (3%)
  between operations  15.8 us (3%)
  blocking collectives  15.2 us (3%)
    all_gather x1, waiting for transfers between devices, on_device(): weights = lax.all_gather(projection, 'zero', axis=0, tiled=True)  115 us
    reduce_scatter x1, waiting for transfers between devices, on_device(): lax.psum_scatter(jnp.einsum('td,tc->dc', grouped_tokens, head_flat, prefe...  34.2 us
    reduce_scatter x1, waiting for transfers between devices, on_device(): lax.psum_scatter(value_grad.astype(jnp.bfloat16), 'zero', scatter_dimensi...  27.4 us
    dot_general x2, matrix products, attend(): jnp.einsum('rhqk,rqhe->rkhe', score_grad, query_block, preferred_element_...  26.2 us
    all_gather x1, waiting for transfers between devices, on_device(): lax.all_gather(by_head[:, 2], 'zero', axis=0, tiled=True)  24.6 us
    dot_general x2, matrix products, attend(): jnp.einsum('rhqk,rkhe->rqhe', score_grad, key_chosen, preferred_element_t...  23 us
    reduce_scatter x1, waiting for transfers between devices, on_device(): lax.psum_scatter(key_grad.astype(jnp.bfloat16), 'zero', scatter_dimension...  22.9 us
    all_gather x1, waiting for transfers between devices, on_device(): lax.all_gather(by_head[:, 1], 'zero', axis=0, tiled=True)  19.3 us
  transfers between devices with their start and end apart: 11, of which 8 were waited for; matrix products, arithmetic and copies ran while one was open for 6% of the time, Pallas kernels for 0%

commit v1 on v0

v1 whole, which is shorter than its diff:
```python
import functools

import jax
import jax.numpy as jnp
from jax import lax
from jax.experimental import pallas as pl
from jax.experimental.pallas import tpu as pltpu
from jax.sharding import PartitionSpec as P

HEADS = 16
HEAD = 64
BLOCK = 128
NBK = 8
MESH = pl.DeviceIdType.MESH
F32 = jnp.float32
BF16 = jnp.bfloat16
VMEM = pl.BlockSpec(memory_space=pltpu.VMEM)
SMEM = pl.BlockSpec(memory_space=pltpu.SMEM)
LIMIT = 56 * 1024 * 1024


def remote(src, dst, send, recv, where):
    return pltpu.make_async_remote_copy(
        src_ref=src, dst_ref=dst, send_sem=send, recv_sem=recv, device_id=where, device_id_type=MESH
    )


def greet(S, Z, sme, zme):
    barrier = pltpu.get_barrier_semaphore()
    for d in range(1, S):
        pl.semaphore_signal(
            barrier, inc=1, device_id=(lax.rem(sme + d, S), zme), device_id_type=MESH
        )
    for d in range(1, Z):
        pl.semaphore_signal(
            barrier, inc=1, device_id=(sme, lax.rem(zme + d, Z)), device_id_type=MESH
        )
    pl.semaphore_wait(barrier, S + Z - 2)


def gather_kernel(
    S, Z, tok_ref, w_ref, up_ref, tokg_ref, wg_ref, q_ref, kv_ref, u_ref,
    ts, tr, ws, wr, us, ur, ks, kr,
):
    sme, zme = lax.axis_index("seq"), lax.axis_index("zero")
    T = tok_ref.shape[0]
    W = w_ref.shape[1]

    def rows(i):
        return pl.ds(pl.multiple_of(i * T, T), T)

    def wrows(i):
        return pl.ds(pl.multiple_of(i * W, W), W)

    def w_copy(d, owner, peer):
        return remote(w_ref, wg_ref.at[:, wrows(owner)], ws.at[d], wr.at[d], (sme, peer))

    def t_copy(d, owner, peer):
        return remote(tok_ref, tokg_ref.at[rows(owner)], ts.at[d], tr.at[d], (peer, zme))

    def u_copy(d, owner, peer, part):
        return remote(up_ref.at[part], u_ref.at[rows(owner)], us.at[d], ur.at[d], (peer, zme))

    def k_copy(zd, d, owner, peer, block):
        at = kv_ref.at[:, owner, rows(block)]
        src = kv_ref.at[:, zme, rows(block)]
        return remote(src, at, ks.at[zd, d], kr.at[zd, d], (sme, peer))

    greet(S, Z, sme, zme)
    for d in range(1, Z):
        w_copy(d, zme, lax.rem(zme + d, Z)).start()
    for d in range(1, S):
        t_copy(d, sme, lax.rem(sme + d, S)).start()
    for d in range(1, S):
        peer = lax.rem(sme + d, S)
        u_copy(d, sme, peer, peer).start()
    wg_ref[:, wrows(zme), :] = w_ref[...]
    tokg_ref[rows(sme), :] = tok_ref[...]
    u_ref[rows(sme), :] = up_ref[sme]
    for d in range(1, Z):
        w_copy(d, lax.rem(zme + Z - d, Z), lax.rem(zme + d, Z)).wait_recv()

    def project(d):
        block = lax.rem(sme + S - d, S)
        here = tokg_ref[rows(block), :]
        q_ref[rows(block), :] = jnp.dot(here, wg_ref[0], preferred_element_type=F32).astype(BF16)
        for i in range(2):
            kv_ref[i, zme, rows(block), :] = jnp.dot(
                here, wg_ref[i + 1], preferred_element_type=F32
            ).astype(BF16)
        for zd in range(1, Z):
            k_copy(zd, d, zme, lax.rem(zme + zd, Z), block).start()

    project(0)

    def step(d, carry):
        t_copy(d, lax.rem(sme + S - d, S), lax.rem(sme + d, S)).wait_recv()
        project(d)
        return carry

    lax.fori_loop(1, S, step, 0)

    def finish(d, carry):
        block = lax.rem(sme + S - d, S)
        for zd in range(1, Z):
            copy = k_copy(zd, d, lax.rem(zme + Z - zd, Z), lax.rem(zme + zd, Z), block)
            copy.wait_recv()
            k_copy(zd, d, zme, lax.rem(zme + zd, Z), block).wait_send()
        return carry

    for d in range(1, S):
        peer = lax.rem(sme + d, S)
        u_copy(d, lax.rem(sme + S - d, S), peer, peer).wait_recv()
        u_copy(d, sme, peer, peer).wait_send()
        t_copy(d, sme, peer).wait_send()
    for d in range(1, Z):
        w_copy(d, zme, lax.rem(zme + d, Z)).wait_send()
    lax.fori_loop(0, S, finish, 0)


def attend_kernel(S, Z, per_shard, pat_ref, q_ref, kv_ref, u_ref, o_ref, dq_ref, dkv_ref, acc):
    zme = lax.axis_index("zero")
    hc = q_ref.shape[1]
    heads = hc // HEAD
    local = S * per_shard
    total = Z * local
    scale = HEAD ** (-0.5)

    def clear(i, carry):
        acc[0, i] = jnp.zeros((BLOCK, hc), F32)
        acc[1, i] = jnp.zeros((BLOCK, hc), F32)
        return carry

    lax.fori_loop(0, total, clear, 0)
    lane = lax.broadcasted_iota(jnp.int32, (BLOCK, hc), 1) // HEAD

    def split(x):
        if heads == 1:
            return x
        return jnp.concatenate([jnp.where(lane == h, x, jnp.zeros_like(x)) for h in range(heads)], axis=0)

    def join(x):
        parts = [
            x[h * HEAD : (h + 1) * HEAD, h * BLOCK : (h + 1) * BLOCK] for h in range(heads)
        ]
        both = parts[0] if heads == 1 else jnp.concatenate(parts, axis=0)
        return both.T.astype(BF16)

    def nt(a, b):
        return lax.dot_general(a, b, (((1,), (1,)), ((), ())), preferred_element_type=F32)

    def tn(a, b):
        return lax.dot_general(a, b, (((0,), (0,)), ((), ())), preferred_element_type=F32)

    def step(r, carry):
        row = (r // per_shard * Z + zme) * per_shard + r % per_shard
        slots = []
        for j in range(NBK):
            b = pat_ref[row, j]
            shard = b // per_shard
            slots.append(shard % Z * local + shard // Z * per_shard + b % per_shard)
        at = pl.ds(pl.multiple_of(r * BLOCK, BLOCK), BLOCK)
        qq = split(q_ref[at, :])
        uu = split(u_ref[at, :])
        keys = jnp.concatenate([kv_ref[0, s] for s in slots], axis=0)
        values = jnp.concatenate([kv_ref[1, s] for s in slots], axis=0)
        scores = nt(keys, qq) * scale
        top = jnp.max(scores, axis=0, keepdims=True)
        exponent = jnp.exp(scores - top)
        prob = exponent * (1.0 / jnp.sum(exponent, axis=0, keepdims=True))
        low = prob.astype(BF16)
        grad = nt(values, uu)
        delta = jnp.sum(prob * grad, axis=0, keepdims=True)
        sg = (prob * (grad - delta) * scale).astype(BF16)
        o_ref[at, :] = join(tn(values, low))
        dq_ref[at, :] = join(tn(keys, sg))
        dk = jnp.dot(sg, qq, preferred_element_type=F32)
        dv = jnp.dot(low, uu, preferred_element_type=F32)
        for j in range(NBK):
            acc[0, slots[j]] += dk[j * BLOCK : (j + 1) * BLOCK]
            acc[1, slots[j]] += dv[j * BLOCK : (j + 1) * BLOCK]
        return carry

    lax.fori_loop(0, local, step, 0)

    def store(i, carry):
        dkv_ref[0, i] = acc[0, i].astype(BF16)
        dkv_ref[1, i] = acc[1, i].astype(BF16)
        return carry

    lax.fori_loop(0, total, store, 0)


def reduce_kernel(
    S, Z, o_ref, dq_ref, dkv_ref, tokg_ref, wg_ref, att_ref, tg_ref, wo_ref,
    kbuf, grads, wacc, wsend, wbuf, town, tsend, tbuf,
    os, orr, ks, kr, ws, wr, ts, tr, gs, gr,
):
    sme, zme = lax.axis_index("seq"), lax.axis_index("zero")
    T = att_ref.shape[1]
    W = wo_ref.shape[2]

    def rows(i):
        return pl.ds(pl.multiple_of(i * T, T), T)

    def wrows(i):
        return pl.ds(pl.multiple_of(i * W, W), W)

    def speer(d):
        return lax.rem(sme + d, S)

    def sfrom(d):
        return lax.rem(sme + S - d, S)

    def zpeer(d):
        return lax.rem(zme + d, Z)

    def k_copy(d):
        return remote(dkv_ref.at[:, zpeer(d)], kbuf.at[d - 1], ks.at[d], kr.at[d], (sme, zpeer(d)))

    def o_copy(d, owner):
        return remote(
            o_ref.at[rows(speer(d))], att_ref.at[owner], os.at[d], orr.at[d], (speer(d), zme)
        )

    def w_copy(d):
        return remote(
            wsend.at[:, wrows(zpeer(d))], wbuf.at[d - 1], ws.at[d], wr.at[d], (sme, zpeer(d))
        )

    def t_copy(d):
        return remote(tsend.at[d - 1], tbuf.at[d - 1], ts.at[d], tr.at[d], (speer(d), zme))

    def g_copy(d, owner):
        return remote(wo_ref.at[sme], wo_ref.at[owner], gs.at[d], gr.at[d], (speer(d), zme))

    def weight_part(i):
        part = lax.dot_general(
            tokg_ref[...], grads[i], (((0,), (0,)), ((), ())), preferred_element_type=F32
        )
        wacc[i] = part
        wsend[i] = part.astype(BF16)

    greet(S, Z, sme, zme)
    for d in range(1, Z):
        k_copy(d).start()
    for d in range(1, S):
        o_copy(d, sme).start()
    att_ref[sme] = o_ref[rows(sme), :]
    grads[0] = dq_ref[...]
    weight_part(0)
    for d in range(1, Z):
        k_copy(d).wait_recv()
    for i in range(2):
        total = dkv_ref[i, zme].astype(F32)
        for d in range(1, Z):
            total += kbuf[d - 1, i].astype(F32)
        grads[i + 1] = total.astype(BF16)
    for i in range(2):
        weight_part(i + 1)
    for d in range(1, Z):
        w_copy(d).start()

    def token_part(block):
        total = None
        for i in range(3):
            part = lax.dot_general(
                grads[i, rows(block), :], wg_ref[i], (((1,), (1,)), ((), ())),
                preferred_element_type=F32,
            )
            total = part if total is None else total + part
        return total

    def send_tokens(d, carry):
        tsend[d - 1] = token_part(speer(d)).astype(BF16)
        t_copy(d).start()
        return carry

    lax.fori_loop(1, S, send_tokens, 0)
    town[...] = token_part(sme)
    for d in range(1, Z):
        w_copy(d).wait_recv()
    for i in range(3):
        total = wacc[i, wrows(zme), :]
        for d in range(1, Z):
            total += wbuf[d - 1, i].astype(F32)
        wo_ref[sme, i] = total.astype(BF16)
    for d in range(1, S):
        g_copy(d, sme).start()

    def add_tokens(d, carry):
        t_copy(d).wait_recv()
        town[...] += tbuf[d - 1].astype(F32)
        return carry

    lax.fori_loop(1, S, add_tokens, 0)
    tg_ref[...] = town[...].astype(BF16)
    for d in range(1, Z):
        k_copy(d).wait_send()
        w_copy(d).wait_send()
    for d in range(1, S):
        o_copy(d, sfrom(d)).wait_recv()
        o_copy(d, sme).wait_send()
        t_copy(d).wait_send()
        g_copy(d, sfrom(d)).wait_recv()
        g_copy(d, sme).wait_send()


def dma(*shape):
    return pltpu.SemaphoreType.DMA(shape)


def on_device(tokens, projection, pattern, upstream):
    S = lax.axis_size("seq")
    Z = lax.axis_size("zero")
    T, D = tokens.shape
    hc = HEADS // S * HEAD
    W = projection.shape[0]
    R = S * T
    per_shard = T // BLOCK
    total = Z * S * per_shard
    shape = jax.ShapeDtypeStruct
    own = lax.dynamic_index_in_dim(
        projection.reshape(W, 3, S, hc), lax.axis_index("seq"), axis=2, keepdims=False
    )
    own = own.transpose(1, 0, 2)
    up = upstream.reshape(T, S, hc).transpose(1, 0, 2)
    tokg, wg, q, kv, u = pl.pallas_call(
        functools.partial(gather_kernel, S, Z),
        out_shape=(
            shape((R, D), BF16), shape((3, D, hc), BF16), shape((R, hc), BF16),
            shape((2, Z, R, hc), BF16), shape((R, hc), BF16),
        ),
        in_specs=[VMEM] * 3,
        out_specs=(VMEM,) * 5,
        scratch_shapes=[
            dma(S), dma(S), dma(Z), dma(Z), dma(S), dma(S), dma(Z, S), dma(Z, S),
        ],
        compiler_params=pltpu.CompilerParams(
            collective_id=0, has_side_effects=True, vmem_limit_bytes=LIMIT
        ),
        name="gather",
    )(tokens, own, up)
    out, dq, dkv = pl.pallas_call(
        functools.partial(attend_kernel, S, Z, per_shard),
        out_shape=(
            shape((R, hc), BF16), shape((R, hc), BF16), shape((2, total, BLOCK, hc), BF16),
        ),
        in_specs=[SMEM] + [VMEM] * 3,
        out_specs=(VMEM,) * 3,
        scratch_shapes=[pltpu.VMEM((2, total, BLOCK, hc), F32)],
        compiler_params=pltpu.CompilerParams(vmem_limit_bytes=LIMIT),
        name="attend",
    )(pattern, q, kv.reshape(2, total, BLOCK, hc), u)
    att, tg, wo = pl.pallas_call(
        functools.partial(reduce_kernel, S, Z),
        out_shape=(
            shape((S, T, hc), BF16), shape((T, D), BF16), shape((S, 3, W, hc), BF16),
        ),
        in_specs=[VMEM] * 5,
        out_specs=(VMEM,) * 3,
        scratch_shapes=[
            pltpu.VMEM((Z - 1, 2, R, hc), BF16),
            pltpu.VMEM((3, R, hc), BF16),
            pltpu.VMEM((3, D, hc), F32),
            pltpu.VMEM((3, D, hc), BF16),
            pltpu.VMEM((Z - 1, 3, W, hc), BF16),
            pltpu.VMEM((T, D), F32),
            pltpu.VMEM((S - 1, T, D), BF16),
            pltpu.VMEM((S - 1, T, D), BF16),
            dma(S), dma(S), dma(Z), dma(Z), dma(Z), dma(Z), dma(S), dma(S), dma(S), dma(S),
        ],
        compiler_params=pltpu.CompilerParams(
            collective_id=1, has_side_effects=True, vmem_limit_bytes=LIMIT
        ),
        name="reduce",
    )(out, dq, dkv.reshape(2, Z, R, hc), tokg, wg)
    attended = att.transpose(1, 0, 2).reshape(T, S * hc)
    weight_gradient = wo.transpose(2, 1, 0, 3).reshape(W, 3 * S * hc).astype(F32)
    return (attended, tg, weight_gradient)


def solution(mesh):
    return jax.shard_map(
        on_device,
        mesh=mesh,
        in_specs=(P(("seq", "zero"), None), P("zero", None), P(), P(("seq", "zero"), None)),
        out_specs=(P(("seq", "zero"), None), P(("seq", "zero"), None), P("zero", None)),
        check_vma=False,
    )
```

time: 541 us -> 208 us (0.38)
  the two profiles are of different devices: /device:TPU:11 before, /device:TPU:27 now
where the time goes in v1:
time: 208 us
  Pallas kernels  191 us (92%)
  local copies, waits for them, and re-layouts  14.8 us (7%)
    pallas_call x1, Pallas kernels, on_device(): pl.pallas_call(functools.partial(reduce_kernel, S, Z), out_shape=(shape((...  105 us
    pallas_call x1, Pallas kernels, on_device(): pl.pallas_call(functools.partial(gather_kernel, S, Z), out_shape=(shape((...  69.9 us
    pallas_call x1, Pallas kernels, on_device(): pl.pallas_call(functools.partial(attend_kernel, S, Z, per_shard), out_sha...  16.3 us
    unnamed x9, local copies, waits for them, and re-layouts  10 us

profile of v1, /device:TPU:27, one launch (start us, length us, event | category | flops | bytes accessed | tf_op | source)
XLA Modules:
  0.0 208.0 jit_solution(4694202295874771282)
XLA Ops:
  0.6 1.4 copy.12.pat_ref
  2.0 1.1 copy.10
  3.1 0.9 copy.11
  4.0 1.7 copy.18
  5.7 0.4 constant_dynamic-slice_fusion
  6.1 0.7 copy.20
  6.8 69.9 %gather.1 = (bf16[1024,1024]{1,0:T(8,128)(2,1)}, bf16[3,1024,128]{2,1,0:T(8,128)(2,1)}, bf16[1024,128]{1,0:T(8,128)(2,1)}, bf16[2,4,1024,128]{3,2,1,0:T(8,128)(2,1)}, bf16[1024,128]{1,0:T(8,128)(2,1)}) custom-call(bf16[128,1024]{1,0:T(8,128)(2,1)} %tok_ref.1, bf16[3,256,128]{2,1,0:T(8,128)(2,1)} %bitcast.25, bf16[8,128,128]{2,1,0:T(8,128)(2,1)} %bitcast.24), custom_call_target="tpu_custom_call" | custom-call | tf_op jit(solution)/shard_map/gather/pallas_call | solution.py:328
  76.7 16.3 %attend.1 = (bf16[1024,128]{1,0:T(8,128)(2,1)}, bf16[1024,128]{1,0:T(8,128)(2,1)}, bf16[2,32,128,128]{3,2,1,0:T(8,128)(2,1)}) custom-call(s32[32,8]{1,0:T(8,128)} %copy.12.pat_ref, bf16[1024,128]{1,0:T(8,128)(2,1)} %get-tuple-element.14.q_ref, bf16[2,32,128,128]{3,2,1,0:T(8,128)(2,1)} %bitcast.19, bf16[1024,128]{1,0:T(8,128)(2,1)} %get-tuple-element.16.u_ref), custom_call_target="tpu_custom_call" | custom-call | tf_op jit(solution)/shard_map/attend/pallas_call | solution.py:344
  93.0 104.6 %reduce.1 = (bf16[8,128,128]{2,1,0:T(8,128)(2,1)}, bf16[128,1024]{1,0:T(8,128)(2,1)}, bf16[8,3,256,128]{3,2,1,0:T(8,128)(2,1)}) custom-call(bf16[1024,128]{1,0:T(8,128)(2,1)} %get-tuple-element.17.o_ref, bf16[1024,128]{1,0:T(8,128)(2,1)} %get-tuple-element.18.dq_ref, bf16[2,4,1024,128]{3,2,1,0:T(8,128)(2,1)} %bitcast.20, ...), custom_call_target="tpu_custom_call" | custom-call | tf_op jit(solution)/shard_map/reduce/pallas_call | solution.py:355
  197.6 1.1 copy.13
  198.7 0.9 copy.15
  199.6 1.7 convert_bitcast_fusion
  201.3 2.3 %copy.14 = f32[256,3,8,128]{0,3,2,1:T(8,128)} copy(f32[256,3,8,128]{3,0,1,2:T(8,128)S(1)} %convert_bitcast_fusion) | data formatting | bytes 6291456 | tf_op jit(solution)/shard_map/convert_element_type | solution.py:379
  203.7 0.0 copy-start
  203.7 3.6 %copy.16 = f32[256,3072]{1,0:T(8,128)} copy(f32[256,3072]{0,1:T(8,128)} %bitcast.17) | data formatting | bytes 6291456
  207.3 0.0 copy-done
  207.3 0.7 copy.22
Async XLA Ops:
  203.7 3.6 %copy-start = (bf16[128,1024]{1,0:T(8,128)(2,1)S(1)}, bf16[128,1024]{1,0:T(8,128)(2,1)}, u32[]{:S(2)}) copy-start(bf16[128,1024]{1,0:T(8,128)(2,1)} %get-tuple-element.32) | copy-start | bytes 786436

commit v2 on v1

v2 whole, which is shorter than its diff:
```python
import functools

import jax
import jax.numpy as jnp
from jax import lax
from jax.experimental import pallas as pl
from jax.experimental.pallas import tpu as pltpu
from jax.sharding import PartitionSpec as P

HEADS = 16
HEAD = 64
BLOCK = 128
NBK = 8
LANES = 128
MESH = pl.DeviceIdType.MESH
F32 = jnp.float32
BF16 = jnp.bfloat16
VMEM = pl.BlockSpec(memory_space=pltpu.VMEM)
SMEM = pl.BlockSpec(memory_space=pltpu.SMEM)
LIMIT = 56 * 1024 * 1024


def remote(src, dst, send, recv, where):
    return pltpu.make_async_remote_copy(
        src_ref=src, dst_ref=dst, send_sem=send, recv_sem=recv, device_id=where, device_id_type=MESH
    )


def greet(S, Z, sme, zme):
    barrier = pltpu.get_barrier_semaphore()
    for d in range(1, S):
        pl.semaphore_signal(
            barrier, inc=1, device_id=(lax.rem(sme + d, S), zme), device_id_type=MESH
        )
    for d in range(1, Z):
        pl.semaphore_signal(
            barrier, inc=1, device_id=(sme, lax.rem(zme + d, Z)), device_id_type=MESH
        )
    pl.semaphore_wait(barrier, S + Z - 2)


def turn(x):
    return pltpu.roll(x.astype(F32), HEAD, 1).astype(BF16)


def first_half(shape):
    return lax.broadcasted_iota(jnp.int32, shape, 1) < HEAD


def gather_kernel(
    S, Z, H, tok_ref, w_ref, up_ref, tokg_ref, wg_ref, kv_ref, qu_ref,
    wown, kvown, quown, ubuf, ts, tr, ws, wr, us, ur, ks, kr, qs, qr,
):
    sme, zme = lax.axis_index("seq"), lax.axis_index("zero")
    hme = lax.rem(zme, H)
    mate = zme + 1 - 2 * hme
    T = tok_ref.shape[0]
    W = wown.shape[1]

    def rows(i):
        return pl.ds(pl.multiple_of(i * T, T), T)

    def wrows(i):
        return pl.ds(pl.multiple_of(i * W, W), W)

    def w_copy(d, owner, peer):
        return remote(wown, wg_ref.at[:, wrows(owner)], ws.at[d], wr.at[d], (sme, peer))

    def t_copy(d, owner, peer):
        return remote(tok_ref, tokg_ref.at[rows(owner)], ts.at[d], tr.at[d], (peer, zme))

    def u_copy(d, owner, peer):
        return remote(up_ref.at[peer], ubuf.at[rows(owner)], us.at[d], ur.at[d], (peer, zme))

    def k_copy(zd, d, owner, peer, block):
        src = kvown.at[lax.rem(peer, H), rows(block)]
        return remote(src, kv_ref.at[owner, rows(block)], ks.at[zd, d], kr.at[zd, d], (sme, peer))

    def q_copy(d, group, block):
        src = quown.at[1 - hme, rows(block)]
        return remote(src, qu_ref.at[group, rows(block)], qs.at[d], qr.at[d], (sme, mate))

    if H == 2:
        half = first_half((W, LANES))
        turned = turn(w_ref[2])
        wown[0] = w_ref[0]
        wown[1] = jnp.where(half, w_ref[1], turned)
        wown[2] = jnp.where(half, turned, w_ref[1])
    else:
        wown[...] = w_ref[...]
    greet(S, Z, sme, zme)
    for d in range(1, Z):
        w_copy(d, zme, lax.rem(zme + d, Z)).start()
    for d in range(1, S):
        peer = lax.rem(sme + d, S)
        t_copy(d, sme, peer).start()
        u_copy(d, sme, peer).start()
    wg_ref[:, wrows(zme), :] = wown[...]
    tokg_ref[rows(sme), :] = tok_ref[...]
    ubuf[rows(sme), :] = up_ref[sme]
    for d in range(1, Z):
        w_copy(d, lax.rem(zme + Z - d, Z), lax.rem(zme + d, Z)).wait_recv()

    def project(d):
        block = lax.rem(sme + S - d, S)
        here = tokg_ref[rows(block), :]
        for h in range(H):
            kvown[h, rows(block), :] = jnp.dot(
                here, wg_ref[h + 1], preferred_element_type=F32
            ).astype(BF16)
        for zd in range(1, Z):
            k_copy(zd, d, zme, lax.rem(zme + zd, Z), block).start()
        kv_ref[zme, rows(block), :] = kvown[hme, rows(block), :]
        queries = jnp.dot(here, wg_ref[0], preferred_element_type=F32).astype(BF16)
        half = first_half((T, LANES))
        if H == 2:
            ups = turn(ubuf[rows(block), :])
            quown[0, rows(block), :] = jnp.where(half, queries, ups)
            quown[1, rows(block), :] = jnp.where(half, ups, queries)
            q_copy(d, hme, block).start()
        else:
            quown[0, rows(block), :] = jnp.where(half, queries, ubuf[rows(block), :])
        qu_ref[hme, rows(block), :] = quown[hme, rows(block), :]

    project(0)

    def step(d, carry):
        owner, peer = lax.rem(sme + S - d, S), lax.rem(sme + d, S)
        t_copy(d, owner, peer).wait_recv()
        u_copy(d, owner, peer).wait_recv()
        project(d)
        return carry

    lax.fori_loop(1, S, step, 0)

    def finish(d, carry):
        block = lax.rem(sme + S - d, S)
        for zd in range(1, Z):
            peer = lax.rem(zme + zd, Z)
            k_copy(zd, d, lax.rem(zme + Z - zd, Z), peer, block).wait_recv()
            k_copy(zd, d, zme, peer, block).wait_send()
        if H == 2:
            q_copy(d, 1 - hme, block).wait_recv()
            q_copy(d, hme, block).wait_send()
        return carry

    for d in range(1, S):
        peer = lax.rem(sme + d, S)
        u_copy(d, sme, peer).wait_send()
        t_copy(d, sme, peer).wait_send()
    for d in range(1, Z):
        w_copy(d, zme, lax.rem(zme + d, Z)).wait_send()
    lax.fori_loop(0, S, finish, 0)


def attend_kernel(S, Z, H, per_shard, pat_ref, qu_ref, kv_ref, do_ref, dkv_ref, acc):
    zme = lax.axis_index("zero")
    hme = zme % H
    local = S * per_shard
    total = Z * local
    scale = HEAD ** (-0.5)

    def clear(i, carry):
        acc[i] = jnp.zeros((BLOCK, LANES), F32)
        return carry

    lax.fori_loop(0, total, clear, 0)
    is_q = lax.broadcasted_iota(jnp.int32, (BLOCK, LANES), 1) // HEAD == hme
    is_dq = lax.broadcasted_iota(jnp.int32, (LANES, BLOCK), 0) // HEAD == hme

    def step(i, carry):
        r = i % local
        row = (r // per_shard * Z + zme - hme + i // local) * per_shard + r % per_shard
        slots = []
        for j in range(NBK):
            b = pat_ref[row, j]
            shard = b // per_shard
            slots.append(shard % Z * local + shard // Z * per_shard + b % per_shard)
        qu = qu_ref[i]
        none = jnp.zeros_like(qu)
        both = jnp.concatenate([jnp.where(is_q, qu, none), jnp.where(is_q, none, qu)], axis=0)
        keys = jnp.concatenate([kv_ref[s] for s in slots], axis=0)
        mixed = lax.dot_general(keys, both, (((1,), (1,)), ((), ())), preferred_element_type=F32)
        scores = mixed[:, :BLOCK] * scale
        grad = mixed[:, BLOCK:]
        top = jnp.max(scores, axis=0, keepdims=True)
        exponent = jnp.exp(scores - top)
        prob = exponent * (1.0 / jnp.sum(exponent, axis=0, keepdims=True))
        delta = jnp.sum(prob * grad, axis=0, keepdims=True)
        sg = (prob * (grad - delta) * scale).astype(BF16)
        pair = jnp.concatenate([sg, prob.astype(BF16)], axis=1)
        outs = lax.dot_general(keys, pair, (((0,), (0,)), ((), ())), preferred_element_type=F32)
        do_ref[i] = jnp.where(is_dq, outs[:, :BLOCK], outs[:, BLOCK:]).T.astype(BF16)
        terms = jnp.dot(pair, both, preferred_element_type=F32)
        for j in range(NBK):
            acc[slots[j]] += terms[j * BLOCK : (j + 1) * BLOCK]
        return carry

    lax.fori_loop(0, H * local, step, 0)

    def store(i, carry):
        dkv_ref[i] = acc[i].astype(BF16)
        return carry

    lax.fori_loop(0, total, store, 0)


def reduce_kernel(
    S, Z, H, do_ref, dkv_ref, tokg_ref, wg_ref, att_ref, tg_ref, wo_ref,
    dbuf, osend, kbuf, grads, wacc, wsend, wbuf, town, tsend, tbuf,
    ds, dr, os, orr, ks, kr, ws, wr, ts, tr, gs, gr,
):
    sme, zme = lax.axis_index("seq"), lax.axis_index("zero")
    hme = lax.rem(zme, H)
    mate = zme + 1 - 2 * hme
    T = att_ref.shape[1]
    W = wo_ref.shape[2]
    R = S * T

    def rows(i):
        return pl.ds(pl.multiple_of(i * T, T), T)

    def wrows(i):
        return pl.ds(pl.multiple_of(i * W, W), W)

    def speer(d):
        return lax.rem(sme + d, S)

    def sfrom(d):
        return lax.rem(sme + S - d, S)

    def zpeer(d):
        return lax.rem(zme + d, Z)

    def d_copy():
        return remote(do_ref.at[1 - hme], dbuf, ds, dr, (sme, mate))

    def k_copy(d):
        return remote(dkv_ref.at[zpeer(d)], kbuf.at[d - 1], ks.at[d], kr.at[d], (sme, zpeer(d)))

    def o_copy(d, owner):
        return remote(
            osend.at[rows(speer(d))], att_ref.at[owner], os.at[d], orr.at[d], (speer(d), zme)
        )

    def w_copy(d):
        return remote(
            wsend.at[:, wrows(zpeer(d))], wbuf.at[d - 1], ws.at[d], wr.at[d], (sme, zpeer(d))
        )

    def t_copy(d):
        return remote(tsend.at[d - 1], tbuf.at[d - 1], ts.at[d], tr.at[d], (speer(d), zme))

    def g_copy(d, owner):
        return remote(wo_ref.at[sme], wo_ref.at[owner], gs.at[d], gr.at[d], (speer(d), zme))

    def weight_part(i):
        part = lax.dot_general(
            tokg_ref[...], grads[i], (((0,), (0,)), ((), ())), preferred_element_type=F32
        )
        wacc[i] = part
        wsend[i] = part.astype(BF16)

    greet(S, Z, sme, zme)
    if H == 2:
        d_copy().start()
    for d in range(1, Z):
        k_copy(d).start()
    half = first_half((R, LANES))
    own = do_ref[hme]
    if H == 2:
        d_copy().wait_recv()
        other = dbuf[...]
        even = jnp.where(hme == 0, own, other)
        odd = jnp.where(hme == 0, other, own)
        grads[0] = jnp.where(half, even, odd)
        osend[...] = turn(jnp.where(half, odd, even))
    else:
        grads[0] = jnp.where(half, own, jnp.zeros_like(own))
        osend[...] = own
    for d in range(1, S):
        o_copy(d, sme).start()
    att_ref[sme] = osend[rows(sme), :]
    weight_part(0)
    for d in range(1, Z):
        k_copy(d).wait_recv()
    for h in range(H):
        total = dkv_ref[zme].astype(F32) if h == 0 else None
        for d in range(1, Z):
            if d % H == h:
                term = kbuf[d - 1].astype(F32)
                total = term if total is None else total + term
        grads[1 + lax.rem(hme + h, H)] = total.astype(BF16)
    for h in range(H):
        weight_part(1 + h)
    for d in range(1, Z):
        w_copy(d).start()

    def token_part(block):
        total = None
        for i in range(1 + H):
            part = lax.dot_general(
                grads[i, rows(block), :], wg_ref[i], (((1,), (1,)), ((), ())),
                preferred_element_type=F32,
            )
            total = part if total is None else total + part
        return total

    def send_tokens(d, carry):
        tsend[d - 1] = token_part(speer(d)).astype(BF16)
        t_copy(d).start()
        return carry

    lax.fori_loop(1, S, send_tokens, 0)
    town[...] = token_part(sme)
    for d in range(1, Z):
        w_copy(d).wait_recv()
    sums = []
    for i in range(1 + H):
        total = wacc[i, wrows(zme), :]
        for d in range(1, Z):
            total += wbuf[d - 1, i].astype(F32)
        sums.append(total)
    if H == 2:
        cut = first_half((W, LANES))
        value = pltpu.roll(jnp.where(cut, sums[2], sums[1]), HEAD, 1)
        sums = [sums[0], jnp.where(cut, sums[1], sums[2]), value]
    for i in range(1 + H):
        wo_ref[sme, i] = sums[i].astype(BF16)
    for d in range(1, S):
        g_copy(d, sme).start()

    def add_tokens(d, carry):
        t_copy(d).wait_recv()
        town[...] += tbuf[d - 1].astype(F32)
        return carry

    lax.fori_loop(1, S, add_tokens, 0)
    tg_ref[...] = town[...].astype(BF16)
    if H == 2:
        d_copy().wait_send()
    for d in range(1, Z):
        k_copy(d).wait_send()
        w_copy(d).wait_send()
    for d in range(1, S):
        o_copy(d, sfrom(d)).wait_recv()
        o_copy(d, sme).wait_send()
        t_copy(d).wait_send()
        g_copy(d, sfrom(d)).wait_recv()
        g_copy(d, sme).wait_send()


def dma(*shape):
    return pltpu.SemaphoreType.DMA(shape)


def on_device(tokens, projection, pattern, upstream):
    S = lax.axis_size("seq")
    Z = lax.axis_size("zero")
    T, D = tokens.shape
    hc = HEADS // S * HEAD
    W = projection.shape[0]
    R = S * T
    per_shard = T // BLOCK
    H = hc // HEAD
    total = Z * S * per_shard
    shape = jax.ShapeDtypeStruct
    own = lax.dynamic_index_in_dim(
        projection.reshape(W, 3, S, hc), lax.axis_index("seq"), axis=2, keepdims=False
    )
    own = own.transpose(1, 0, 2)
    up = upstream.reshape(T, S, hc).transpose(1, 0, 2)
    if H == 1:
        own = jnp.stack(
            [
                jnp.concatenate([own[0], jnp.zeros_like(own[0])], axis=1),
                jnp.concatenate([own[1], own[2]], axis=1),
            ]
        )
        up = jnp.concatenate([jnp.zeros_like(up), up], axis=2)
    tokg, wg, kv, qu = pl.pallas_call(
        functools.partial(gather_kernel, S, Z, H),
        out_shape=(
            shape((R, D), BF16), shape((1 + H, D, LANES), BF16),
            shape((Z, R, LANES), BF16), shape((H, R, LANES), BF16),
        ),
        in_specs=[VMEM] * 3,
        out_specs=(VMEM,) * 4,
        scratch_shapes=[
            pltpu.VMEM((1 + H, W, LANES), BF16),
            pltpu.VMEM((H, R, LANES), BF16),
            pltpu.VMEM((H, R, LANES), BF16),
            pltpu.VMEM((R, LANES), BF16),
            dma(S), dma(S), dma(Z), dma(Z), dma(S), dma(S), dma(Z, S), dma(Z, S), dma(S), dma(S),
        ],
        compiler_params=pltpu.CompilerParams(
            collective_id=0, has_side_effects=True, vmem_limit_bytes=LIMIT
        ),
        name="gather",
    )(tokens, own, up)
    do, dkv = pl.pallas_call(
        functools.partial(attend_kernel, S, Z, H, per_shard),
        out_shape=(
            shape((H * S * per_shard, BLOCK, LANES), BF16), shape((total, BLOCK, LANES), BF16),
        ),
        in_specs=[SMEM] + [VMEM] * 2,
        out_specs=(VMEM,) * 2,
        scratch_shapes=[pltpu.VMEM((total, BLOCK, LANES), F32)],
        compiler_params=pltpu.CompilerParams(vmem_limit_bytes=LIMIT),
        name="attend",
    )(
        pattern,
        qu.reshape(H * S * per_shard, BLOCK, LANES),
        kv.reshape(total, BLOCK, LANES),
    )
    att, tg, wo = pl.pallas_call(
        functools.partial(reduce_kernel, S, Z, H),
        out_shape=(
            shape((S, T, LANES), BF16), shape((T, D), BF16), shape((S, 1 + H, W, LANES), BF16),
        ),
        in_specs=[VMEM] * 4,
        out_specs=(VMEM,) * 3,
        scratch_shapes=[
            pltpu.VMEM((R, LANES), BF16),
            pltpu.VMEM((R, LANES), BF16),
            pltpu.VMEM((Z - 1, R, LANES), BF16),
            pltpu.VMEM((1 + H, R, LANES), BF16),
            pltpu.VMEM((1 + H, D, LANES), F32),
            pltpu.VMEM((1 + H, D, LANES), BF16),
            pltpu.VMEM((Z - 1, 1 + H, W, LANES), BF16),
            pltpu.VMEM((T, D), F32),
            pltpu.VMEM((S - 1, T, D), BF16),
            pltpu.VMEM((S - 1, T, D), BF16),
            pltpu.SemaphoreType.DMA, pltpu.SemaphoreType.DMA,
            dma(S), dma(S), dma(Z), dma(Z), dma(Z), dma(Z), dma(S), dma(S), dma(S), dma(S),
        ],
        compiler_params=pltpu.CompilerParams(
            collective_id=1, has_side_effects=True, vmem_limit_bytes=LIMIT
        ),
        name="reduce",
    )(do.reshape(H, R, LANES), dkv.reshape(Z, R, LANES), tokg, wg)
    if H == 1:
        att = att[:, :, HEAD:]
        wo = jnp.stack([wo[:, 0, :, :HEAD], wo[:, 1, :, :HEAD], wo[:, 1, :, HEAD:]], axis=1)
    attended = att.transpose(1, 0, 2).reshape(T, S * hc)
    weight_gradient = wo.transpose(2, 1, 0, 3).reshape(W, 3 * S * hc).astype(F32)
    return (attended, tg, weight_gradient)


def solution(mesh):
    return jax.shard_map(
        on_device,
        mesh=mesh,
        in_specs=(P(("seq", "zero"), None), P("zero", None), P(), P(("seq", "zero"), None)),
        out_specs=(P(("seq", "zero"), None), P(("seq", "zero"), None), P("zero", None)),
        check_vma=False,
    )
```

time: 208 us -> 166 us (0.80)
  the two profiles are of different devices: /device:TPU:27 before, /device:TPU:11 now
where the time goes in v2:
time: 166 us; the launch traced here: 164 us
  Pallas kernels  147 us (89%)
  local copies, waits for them, and re-layouts  14.8 us (9%)
  other arithmetic  1.75 us (1%)
    pallas_call x1, Pallas kernels, on_device(): pl.pallas_call(functools.partial(reduce_kernel, S, Z, H), out_shape=(shap...  77.8 us
    pallas_call x1, Pallas kernels, on_device(): pl.pallas_call(functools.partial(gather_kernel, S, Z, H), out_shape=(shap...  45.5 us
    pallas_call x1, Pallas kernels, on_device(): pl.pallas_call(functools.partial(attend_kernel, S, Z, H, per_shard), out_...  23.7 us
    unnamed x9, local copies, waits for them, and re-layouts  10 us

profile of v2, /device:TPU:11, one launch (start us, length us, event | category | flops | bytes accessed | tf_op | source)
XLA Modules:
  0.0 164.2 jit_solution(843069896865993088)
XLA Ops:
  0.6 1.4 copy.12.pat_ref
  2.0 1.1 copy.10
  3.1 0.9 copy.11
  4.0 1.7 %copy.18 = bf16[32,8,24,128]{3,2,1,0:T(8,128)(2,1)S(1)} copy(bf16[32,8,24,128]{3,1,2,0:T(8,128)(2,1)} %bitcast.21) | data formatting | bytes 3145728
  5.7 0.4 constant_dynamic-slice_fusion
  6.1 0.7 copy.20
  6.8 45.5 %gather.1 = (bf16[1024,1024]{1,0:T(8,128)(2,1)}, bf16[3,1024,128]{2,1,0:T(8,128)(2,1)}, bf16[4,1024,128]{2,1,0:T(8,128)(2,1)}, bf16[2,1024,128]{2,1,0:T(8,128)(2,1)}) custom-call(bf16[128,1024]{1,0:T(8,128)(2,1)} %tok_ref.1, bf16[3,256,128]{2,1,0:T(8,128)(2,1)} %bitcast.27, bf16[8,128,128]{2,1,0:T(8,128)(2,1)} %bitcast.26), custom_call_target="tpu_custom_call" | custom-call | tf_op jit(solution)/shard_map/gather/pallas_call | solution.py:381
  52.3 23.7 %attend.1 = (bf16[16,128,128]{2,1,0:T(8,128)(2,1)}, bf16[32,128,128]{2,1,0:T(8,128)(2,1)}) custom-call(s32[32,8]{1,0:T(8,128)} %copy.12.pat_ref, bf16[16,128,128]{2,1,0:T(8,128)(2,1)} %bitcast.29, bf16[32,128,128]{2,1,0:T(8,128)(2,1)} %bitcast.23), custom_call_target="tpu_custom_call" | custom-call | tf_op jit(solution)/shard_map/attend/pallas_call | solution.py:401
  76.0 77.8 %reduce.1 = (bf16[8,128,128]{2,1,0:T(8,128)(2,1)}, bf16[128,1024]{1,0:T(8,128)(2,1)}, bf16[8,3,256,128]{3,2,1,0:T(8,128)(2,1)}) custom-call(bf16[2,1024,128]{2,1,0:T(8,128)(2,1)} %bitcast.28, bf16[4,1024,128]{2,1,0:T(8,128)(2,1)} %bitcast.22, bf16[1024,1024]{1,0:T(8,128)(2,1)} %get-tuple-element.16.tokg_ref, bf16[3,1024,128]{2,1,0:T(8,128)(2,1)} %get-tuple-element.17.wg_ref), custom_call_target="tpu_custom_call" | custom-call | tf_op jit(solution)/shard_map/reduce/pallas_call | solution.py:416
  153.8 1.1 copy.13
  154.9 0.9 copy.15
  155.8 1.7 %convert_bitcast_fusion = f32[256,3,8,128]{3,0,1,2:T(8,128)S(1)} fusion(bf16[8,3,256,128]{3,2,1,0:T(8,128)(2,1)} %get-tuple-element.20), kind=kLoop, calls=%fused_computation | loop fusion | flops 786432 | bytes 4718592 | tf_op jit(solution)/shard_map/convert_element_type | solution.py:446
  157.5 2.3 %copy.14 = f32[256,3,8,128]{0,3,2,1:T(8,128)} copy(f32[256,3,8,128]{3,0,1,2:T(8,128)S(1)} %convert_bitcast_fusion) | data formatting | bytes 6291456 | tf_op jit(solution)/shard_map/convert_element_type | solution.py:446
  159.9 0.0 copy-start
  159.9 3.6 %copy.16 = f32[256,3072]{1,0:T(8,128)} copy(f32[256,3072]{0,1:T(8,128)} %bitcast.19) | data formatting | bytes 6291456
  163.5 0.0 copy-done
  163.5 0.7 copy.22
Async XLA Ops:
  159.9 3.6 %copy-start = (bf16[128,1024]{1,0:T(8,128)(2,1)S(1)}, bf16[128,1024]{1,0:T(8,128)(2,1)}, u32[]{:S(2)}) copy-start(bf16[128,1024]{1,0:T(8,128)(2,1)} %get-tuple-element.28) | copy-start | bytes 786436

commit v3 on v2

--- a/solution.py
+++ b/solution.py
@@ -49,7 +49,7 @@
 
 def gather_kernel(
     S, Z, H, tok_ref, w_ref, up_ref, tokg_ref, wg_ref, kv_ref, qu_ref,
-    wown, kvown, quown, ubuf, ts, tr, ws, wr, us, ur, ks, kr, qs, qr,
+    wraw, wsem, wown, kvown, quown, ubuf, ts, tr, ws, wr, us, ur, ks, kr, qs, qr,
 ):
     sme, zme = lax.axis_index("seq"), lax.axis_index("zero")
     hme = lax.rem(zme, H)
@@ -63,6 +63,15 @@
     def wrows(i):
         return pl.ds(pl.multiple_of(i * W, W), W)
 
+    def up_part(peer):
+        if H == 1:
+            return up_ref.at[peer]
+        return up_ref.at[:, pl.ds(pl.multiple_of(peer * LANES, LANES), LANES)]
+
+    def raw_copy(i):
+        at = pl.ds(pl.multiple_of((i * S + sme) * LANES, LANES), LANES)
+        return pltpu.make_async_copy(w_ref.at[:, at], wraw.at[i], wsem.at[i])
+
     def w_copy(d, owner, peer):
         return remote(wown, wg_ref.at[:, wrows(owner)], ws.at[d], wr.at[d], (sme, peer))
 
@@ -70,7 +79,7 @@
         return remote(tok_ref, tokg_ref.at[rows(owner)], ts.at[d], tr.at[d], (peer, zme))
 
     def u_copy(d, owner, peer):
-        return remote(up_ref.at[peer], ubuf.at[rows(owner)], us.at[d], ur.at[d], (peer, zme))
+        return remote(up_part(peer), ubuf.at[rows(owner)], us.at[d], ur.at[d], (peer, zme))
 
     def k_copy(zd, d, owner, peer, block):
         src = kvown.at[lax.rem(peer, H), rows(block)]
@@ -81,11 +90,15 @@
         return remote(src, qu_ref.at[group, rows(block)], qs.at[d], qr.at[d], (sme, mate))
 
     if H == 2:
+        for i in range(3):
+            raw_copy(i).start()
+        for i in range(3):
+            raw_copy(i).wait()
         half = first_half((W, LANES))
-        turned = turn(w_ref[2])
-        wown[0] = w_ref[0]
-        wown[1] = jnp.where(half, w_ref[1], turned)
-        wown[2] = jnp.where(half, turned, w_ref[1])
+        turned = turn(wraw[2])
+        wown[0] = wraw[0]
+        wown[1] = jnp.where(half, wraw[1], turned)
+        wown[2] = jnp.where(half, turned, wraw[1])
     else:
         wown[...] = w_ref[...]
     greet(S, Z, sme, zme)
@@ -97,7 +110,10 @@
         u_copy(d, sme, peer).start()
     wg_ref[:, wrows(zme), :] = wown[...]
     tokg_ref[rows(sme), :] = tok_ref[...]
-    ubuf[rows(sme), :] = up_ref[sme]
+    if H == 1:
+        ubuf[rows(sme), :] = up_ref[sme]
+    else:
+        ubuf[rows(sme), :] = up_ref[:, pl.ds(pl.multiple_of(sme * LANES, LANES), LANES)]
     for d in range(1, Z):
         w_copy(d, lax.rem(zme + Z - d, Z), lax.rem(zme + d, Z)).wait_recv()
 
@@ -206,16 +222,21 @@
 
 
 def reduce_kernel(
-    S, Z, H, do_ref, dkv_ref, tokg_ref, wg_ref, att_ref, tg_ref, wo_ref,
-    dbuf, osend, kbuf, grads, wacc, wsend, wbuf, town, tsend, tbuf,
-    ds, dr, os, orr, ks, kr, ws, wr, ts, tr, gs, gr,
+    S, Z, H, do_ref, dkv_ref, tokg_ref, wg_ref, att_ref, tg_ref, wout_ref,
+    dbuf, osend, kbuf, grads, wacc, wsend, wbuf, wo, att, part, csend, cbuf, tsend, tbuf,
+    ds, dr, os, orr, ks, kr, ws, wr, cs, cr, ts, tr, gs, gr, fs, fr,
 ):
     sme, zme = lax.axis_index("seq"), lax.axis_index("zero")
     hme = lax.rem(zme, H)
     mate = zme + 1 - 2 * hme
-    T = att_ref.shape[1]
-    W = wo_ref.shape[2]
+    C = S // 2
+    core = lax.rem(sme, 2)
+    chip = sme // 2
+    twin = sme + 1 - 2 * core
+    T = tg_ref.shape[0]
+    W = wo.shape[2]
     R = S * T
+    hc = H * HEAD
 
     def rows(i):
         return pl.ds(pl.multiple_of(i * T, T), T)
@@ -238,21 +259,45 @@
     def k_copy(d):
         return remote(dkv_ref.at[zpeer(d)], kbuf.at[d - 1], ks.at[d], kr.at[d], (sme, zpeer(d)))
 
+    def there(d):
+        return lax.rem(chip + d, C)
+
+    def back(d):
+        return lax.rem(chip + C - d, C)
+
     def o_copy(d, owner):
         return remote(
-            osend.at[rows(speer(d))], att_ref.at[owner], os.at[d], orr.at[d], (speer(d), zme)
-        )
-
-    def w_copy(d):
+            osend.at[rows(speer(d))], att.at[owner], os.at[d], orr.at[d], (speer(d), zme)
+        )
+
+    def w_copy(d, i):
         return remote(
-            wsend.at[:, wrows(zpeer(d))], wbuf.at[d - 1], ws.at[d], wr.at[d], (sme, zpeer(d))
-        )
+            wsend.at[i, wrows(zpeer(d))], wbuf.at[d - 1, i], ws.at[d, i], wr.at[d, i],
+            (sme, zpeer(d)),
+        )
+
+    def c_copy(d):
+        return remote(csend.at[d], cbuf.at[d], cs.at[d], cr.at[d], (twin, zme))
 
     def t_copy(d):
-        return remote(tsend.at[d - 1], tbuf.at[d - 1], ts.at[d], tr.at[d], (speer(d), zme))
-
-    def g_copy(d, owner):
-        return remote(wo_ref.at[sme], wo_ref.at[owner], gs.at[d], gr.at[d], (speer(d), zme))
+        return remote(
+            tsend.at[d - 1], tbuf.at[d - 1], ts.at[d], tr.at[d], (there(d) * 2 + core, zme)
+        )
+
+    def span(k):
+        return pl.ds(0, 1) if k == 0 else pl.ds(1, wo.shape[1] - 1)
+
+    def g_copy(k, d, owner):
+        block = wo.at[sme, span(k)]
+        return remote(
+            block, wo.at[owner, span(k)], gs.at[k, d], gr.at[k, d], (there(d) * 2 + core, zme)
+        )
+
+    def f_copy(k, d, side):
+        block = wo.at[back(d) * 2 + core, span(k)]
+        return remote(
+            block, wo.at[back(d) * 2 + side, span(k)], fs.at[k, d], fr.at[k, d], (twin, zme)
+        )
 
     def weight_part(i):
         part = lax.dot_general(
@@ -280,8 +325,10 @@
         osend[...] = own
     for d in range(1, S):
         o_copy(d, sme).start()
-    att_ref[sme] = osend[rows(sme), :]
+    att[sme] = osend[rows(sme), :]
     weight_part(0)
+    for d in range(1, Z):
+        w_copy(d, 0).start()
     for d in range(1, Z):
         k_copy(d).wait_recv()
     for h in range(H):
@@ -293,61 +340,109 @@
         grads[1 + lax.rem(hme + h, H)] = total.astype(BF16)
     for h in range(H):
         weight_part(1 + h)
-    for d in range(1, Z):
-        w_copy(d).start()
+        for d in range(1, Z):
+            w_copy(d, 1 + h).start()
+
+    def weight_sum(i):
+        for d in range(1, Z):
+            w_copy(d, i).wait_recv()
+        total = wacc[i, wrows(zme), :]
+        for d in range(1, Z):
+            total += wbuf[d - 1, i].astype(F32)
+        return total
+
+    def share(k):
+        for d in range(1, C):
+            g_copy(k, d, sme).start()
+        f_copy(k, 0, core).start()
+
+    def forward(k):
+        for d in range(1, C):
+            g_copy(k, d, back(d) * 2 + core).wait_recv()
+            f_copy(k, d, core).start()
+
+    wo[sme, 0] = weight_sum(0).astype(BF16)
+    share(0)
 
     def token_part(block):
         total = None
         for i in range(1 + H):
-            part = lax.dot_general(
+            term = lax.dot_general(
                 grads[i, rows(block), :], wg_ref[i], (((1,), (1,)), ((), ())),
                 preferred_element_type=F32,
             )
-            total = part if total is None else total + part
+            total = term if total is None else total + term
         return total
 
-    def send_tokens(d, carry):
-        tsend[d - 1] = token_part(speer(d)).astype(BF16)
+    def twin_part(j, carry):
+        d = lax.rem(j + 1, C)
+        csend[d] = token_part(there(d) * 2 + 1 - core).astype(BF16)
+        c_copy(d).start()
+        return carry
+
+    lax.fori_loop(0, C, twin_part, 0)
+
+    def own_part(d, carry):
+        total = token_part(there(d) * 2 + core)
+        c_copy(d).wait_recv()
+        tsend[d - 1] = (total + cbuf[d].astype(F32)).astype(BF16)
         t_copy(d).start()
         return carry
 
-    lax.fori_loop(1, S, send_tokens, 0)
-    town[...] = token_part(sme)
-    for d in range(1, Z):
-        w_copy(d).wait_recv()
-    sums = []
-    for i in range(1 + H):
-        total = wacc[i, wrows(zme), :]
-        for d in range(1, Z):
-            total += wbuf[d - 1, i].astype(F32)
-        sums.append(total)
+    lax.fori_loop(1, C, own_part, 0)
+    part[...] = token_part(sme)
+    c_copy(0).wait_recv()
+    part[...] += cbuf[0].astype(F32)
+    forward(0)
+    sums = [weight_sum(1 + h) for h in range(H)]
     if H == 2:
         cut = first_half((W, LANES))
-        value = pltpu.roll(jnp.where(cut, sums[2], sums[1]), HEAD, 1)
-        sums = [sums[0], jnp.where(cut, sums[1], sums[2]), value]
-    for i in range(1 + H):
-        wo_ref[sme, i] = sums[i].astype(BF16)
+        value = pltpu.roll(jnp.where(cut, sums[1], sums[0]), HEAD, 1)
+        sums = [jnp.where(cut, sums[0], sums[1]), value]
+    for h in range(H):
+        wo[sme, 1 + h] = sums[h].astype(BF16)
+    share(1)
+    for d in range(1, C):
+        t_copy(d).wait_recv()
+        part[...] += tbuf[d - 1].astype(F32)
+    tg_ref[...] = part[...].astype(BF16)
     for d in range(1, S):
-        g_copy(d, sme).start()
-
-    def add_tokens(d, carry):
-        t_copy(d).wait_recv()
-        town[...] += tbuf[d - 1].astype(F32)
-        return carry
-
-    lax.fori_loop(1, S, add_tokens, 0)
-    tg_ref[...] = town[...].astype(BF16)
+        o_copy(d, sfrom(d)).wait_recv()
+    for p in range(S):
+        block = att[p]
+        att_ref[:, p * hc : (p + 1) * hc] = block if H == 2 else block[:, HEAD:]
+    forward(1)
+    for k in range(2):
+        for d in range(C):
+            f_copy(k, d, 1 - core).wait_recv()
+        for p in range(S):
+            for i in range(3) if H == 2 else ():
+                if (k == 0) == (i == 0):
+                    lo = (i * S + p) * hc
+                    wout_ref[:, lo : lo + hc] = wo[p, i].astype(F32)
+    if H == 1:
+        for p in range(S):
+            both = wo[p, 1].astype(F32)
+            three = [wo[p, 0].astype(F32)[:, :HEAD], both[:, :HEAD], both[:, HEAD:]]
+            for i in range(3):
+                lo = (i * S + p) * hc
+                wout_ref[:, lo : lo + hc] = three[i]
     if H == 2:
         d_copy().wait_send()
     for d in range(1, Z):
         k_copy(d).wait_send()
-        w_copy(d).wait_send()
+        for i in range(1 + H):
+            w_copy(d, i).wait_send()
     for d in range(1, S):
-        o_copy(d, sfrom(d)).wait_recv()
         o_copy(d, sme).wait_send()
-        t_copy(d).wait_send()
-        g_copy(d, sfrom(d)).wait_recv()
-        g_copy(d, sme).wait_send()
+    for d in range(C):
+        c_copy(d).wait_send()
+        for k in range(2):
+            f_copy(k, d, core).wait_send()
+        if d:
+            t_copy(d).wait_send()
+            for k in range(2):
+                g_copy(k, d, sme).wait_send()
 
 
 def dma(*shape):
@@ -365,12 +460,13 @@
     H = hc // HEAD
     total = Z * S * per_shard
     shape = jax.ShapeDtypeStruct
-    own = lax.dynamic_index_in_dim(
-        projection.reshape(W, 3, S, hc), lax.axis_index("seq"), axis=2, keepdims=False
-    )
-    own = own.transpose(1, 0, 2)
-    up = upstream.reshape(T, S, hc).transpose(1, 0, 2)
+    own, up = projection, upstream
     if H == 1:
+        own = lax.dynamic_index_in_dim(
+            projection.reshape(W, 3, S, hc), lax.axis_index("seq"), axis=2, keepdims=False
+        )
+        own = own.transpose(1, 0, 2)
+        up = upstream.reshape(T, S, hc).transpose(1, 0, 2)
         own = jnp.stack(
             [
                 jnp.concatenate([own[0], jnp.zeros_like(own[0])], axis=1),
@@ -384,9 +480,11 @@
             shape((R, D), BF16), shape((1 + H, D, LANES), BF16),
             shape((Z, R, LANES), BF16), shape((H, R, LANES), BF16),
         ),
-        in_specs=[VMEM] * 3,
+        in_specs=[VMEM, pl.BlockSpec(memory_space=pl.ANY) if H == 2 else VMEM, VMEM],
         out_specs=(VMEM,) * 4,
         scratch_shapes=[
+            pltpu.VMEM((3, W, LANES), BF16),
+            dma(3),
             pltpu.VMEM((1 + H, W, LANES), BF16),
             pltpu.VMEM((H, R, LANES), BF16),
             pltpu.VMEM((H, R, LANES), BF16),
@@ -416,7 +514,7 @@
     att, tg, wo = pl.pallas_call(
         functools.partial(reduce_kernel, S, Z, H),
         out_shape=(
-            shape((S, T, LANES), BF16), shape((T, D), BF16), shape((S, 1 + H, W, LANES), BF16),
+            shape((T, S * hc), BF16), shape((T, D), BF16), shape((W, 3 * S * hc), F32),
         ),
         in_specs=[VMEM] * 4,
         out_specs=(VMEM,) * 3,
@@ -428,23 +526,24 @@
             pltpu.VMEM((1 + H, D, LANES), F32),
             pltpu.VMEM((1 + H, D, LANES), BF16),
             pltpu.VMEM((Z - 1, 1 + H, W, LANES), BF16),
+            pltpu.VMEM((S, 1 + H, W, LANES), BF16),
+            pltpu.VMEM((S, T, LANES), BF16),
             pltpu.VMEM((T, D), F32),
-            pltpu.VMEM((S - 1, T, D), BF16),
-            pltpu.VMEM((S - 1, T, D), BF16),
+            pltpu.VMEM((S // 2, T, D), BF16),
+            pltpu.VMEM((S // 2, T, D), BF16),
+            pltpu.VMEM((S // 2 - 1, T, D), BF16),
+            pltpu.VMEM((S // 2 - 1, T, D), BF16),
             pltpu.SemaphoreType.DMA, pltpu.SemaphoreType.DMA,
-            dma(S), dma(S), dma(Z), dma(Z), dma(Z), dma(Z), dma(S), dma(S), dma(S), dma(S),
+            dma(S), dma(S), dma(Z), dma(Z), dma(Z, 1 + H), dma(Z, 1 + H),
+            dma(S // 2), dma(S // 2), dma(S // 2), dma(S // 2),
+            dma(2, S // 2), dma(2, S // 2), dma(2, S // 2), dma(2, S // 2),
         ],
         compiler_params=pltpu.CompilerParams(
             collective_id=1, has_side_effects=True, vmem_limit_bytes=LIMIT
         ),
         name="reduce",
     )(do.reshape(H, R, LANES), dkv.reshape(Z, R, LANES), tokg, wg)
-    if H == 1:
-        att = att[:, :, HEAD:]
-        wo = jnp.stack([wo[:, 0, :, :HEAD], wo[:, 1, :, :HEAD], wo[:, 1, :, HEAD:]], axis=1)
-    attended = att.transpose(1, 0, 2).reshape(T, S * hc)
-    weight_gradient = wo.transpose(2, 1, 0, 3).reshape(W, 3 * S * hc).astype(F32)
-    return (attended, tg, weight_gradient)
+    return (att, tg, wo)
 
 
 def solution(mesh):

time: 166 us -> 150 us (0.904); the launches traced: 164 us -> 150 us
  local copies, waits for them, and re-layouts: 14.8 us -> 8.6 us
  Pallas kernels: 147 us -> 141 us
  other arithmetic: 1.75 us -> 0 us
    pallas_call x1, Pallas kernels: 77.8 us -> 70.8 us  [on_device(): pl.pallas_call(functools.partial(reduce_kernel, S, Z, H), out_shape=(shap...]
    convert_element_type x1 -> x0, local copies, waits for them, and re-layouts: 2.34 us -> none  [on_device(): wo.transpose(2, 1, 0, 3).reshape(W, 3 * S * hc).astype(F32)]
    convert_element_type x1 -> x0, other arithmetic: 1.75 us -> none  [on_device(): wo.transpose(2, 1, 0, 3).reshape(W, 3 * S * hc).astype(F32)]
    unnamed x9 -> x4, local copies, waits for them, and re-layouts: 10 us -> 8.6 us
where the time goes in v3:
time: 150 us
  Pallas kernels  141 us (94%)
  local copies, waits for them, and re-layouts  8.6 us (6%)
    pallas_call x1, Pallas kernels, on_device(): pl.pallas_call(functools.partial(reduce_kernel, S, Z, H), out_shape=(shap...  70.8 us
    pallas_call x1, Pallas kernels, on_device(): pl.pallas_call(functools.partial(gather_kernel, S, Z, H), out_shape=(shap...  46.3 us
    pallas_call x1, Pallas kernels, on_device(): pl.pallas_call(functools.partial(attend_kernel, S, Z, H, per_shard), out_...  23.7 us
    unnamed x4, local copies, waits for them, and re-layouts  8.6 us

profile of v3, /device:TPU:11, one launch (start us, length us, event | category | flops | bytes accessed | tf_op | source)
XLA Modules:
  0.0 150.0 jit_solution(10818756439633150979)
XLA Ops:
  0.6 1.4 copy.7.pat_ref
  2.0 46.3 %gather.1 = (bf16[1024,1024]{1,0:T(8,128)(2,1)}, bf16[3,1024,128]{2,1,0:T(8,128)(2,1)}, bf16[4,1024,128]{2,1,0:T(8,128)(2,1)}, bf16[2,1024,128]{2,1,0:T(8,128)(2,1)}) custom-call(bf16[128,1024]{1,0:T(8,128)(2,1)} %tok_ref.1, bf16[256,3072]{1,0:T(8,128)(2,1)} %w_ref.1, bf16[128,1024]{1,0:T(8,128)(2,1)} %up_ref.1), custom_call_target="tpu_custom_call" | custom-call | tf_op jit(solution)/shard_map/gather/pallas_call | solution.py:477
  48.3 23.7 %attend.1 = (bf16[16,128,128]{2,1,0:T(8,128)(2,1)}, bf16[32,128,128]{2,1,0:T(8,128)(2,1)}) custom-call(s32[32,8]{1,0:T(8,128)} %copy.7.pat_ref, bf16[16,128,128]{2,1,0:T(8,128)(2,1)} %bitcast.7, bf16[32,128,128]{2,1,0:T(8,128)(2,1)} %bitcast.5), custom_call_target="tpu_custom_call" | custom-call | tf_op jit(solution)/shard_map/attend/pallas_call | solution.py:499
  72.0 70.8 %reduce.1 = (bf16[128,1024]{1,0:T(8,128)(2,1)}, bf16[128,1024]{1,0:T(8,128)(2,1)}, f32[256,3072]{1,0:T(8,128)}) custom-call(bf16[2,1024,128]{2,1,0:T(8,128)(2,1)} %bitcast.6, bf16[4,1024,128]{2,1,0:T(8,128)(2,1)} %bitcast.4, bf16[1024,1024]{1,0:T(8,128)(2,1)} %get-tuple-element.13.tokg_ref, bf16[3,1024,128]{2,1,0:T(8,128)(2,1)} %get-tuple-element.14.wg_ref), custom_call_target="tpu_custom_call" | custom-call | tf_op jit(solution)/shard_map/reduce/pallas_call | solution.py:514
  142.8 1.7 %copy.11 = bf16[128,1024]{1,0:T(8,128)(2,1)} copy(bf16[128,1024]{1,0:T(8,128)(2,1)} %get-tuple-element.18) | data formatting | bytes 524288
  144.4 1.7 %copy.12 = bf16[128,1024]{1,0:T(8,128)(2,1)} copy(bf16[128,1024]{1,0:T(8,128)(2,1)} %get-tuple-element.19) | data formatting | bytes 524288
  146.1 3.9 %copy.13 = f32[256,3072]{1,0:T(8,128)} copy(f32[256,3072]{1,0:T(8,128)} %get-tuple-element.20) | data formatting | bytes 6291456

commit v4 on v3

--- a/solution.py
+++ b/solution.py
@@ -184,7 +184,10 @@
     is_q = lax.broadcasted_iota(jnp.int32, (BLOCK, LANES), 1) // HEAD == hme
     is_dq = lax.broadcasted_iota(jnp.int32, (LANES, BLOCK), 0) // HEAD == hme
 
-    def step(i, carry):
+    def nt(x, y):
+        return lax.dot_general(x, y, (((1,), (1,)), ((), ())), preferred_element_type=F32)
+
+    def begin(i):
         r = i % local
         row = (r // per_shard * Z + zme - hme + i // local) * per_shard + r % per_shard
         slots = []
@@ -196,23 +199,37 @@
         none = jnp.zeros_like(qu)
         both = jnp.concatenate([jnp.where(is_q, qu, none), jnp.where(is_q, none, qu)], axis=0)
         keys = jnp.concatenate([kv_ref[s] for s in slots], axis=0)
-        mixed = lax.dot_general(keys, both, (((1,), (1,)), ((), ())), preferred_element_type=F32)
+        return slots, both, keys, nt(keys, both)
+
+    def soften(mixed):
         scores = mixed[:, :BLOCK] * scale
         grad = mixed[:, BLOCK:]
         top = jnp.max(scores, axis=0, keepdims=True)
         exponent = jnp.exp(scores - top)
-        prob = exponent * (1.0 / jnp.sum(exponent, axis=0, keepdims=True))
-        delta = jnp.sum(prob * grad, axis=0, keepdims=True)
-        sg = (prob * (grad - delta) * scale).astype(BF16)
-        pair = jnp.concatenate([sg, prob.astype(BF16)], axis=1)
+        inverse = 1.0 / jnp.sum(exponent, axis=0, keepdims=True)
+        delta = jnp.sum(exponent * grad, axis=0, keepdims=True) * inverse
+        low = (exponent * inverse).astype(BF16)
+        sg = (exponent * (inverse * scale) * (grad - delta)).astype(BF16)
+        return jnp.concatenate([sg, low], axis=1)
+
+    def end(i, slots, both, keys, pair):
         outs = lax.dot_general(keys, pair, (((0,), (0,)), ((), ())), preferred_element_type=F32)
         do_ref[i] = jnp.where(is_dq, outs[:, :BLOCK], outs[:, BLOCK:]).T.astype(BF16)
         terms = jnp.dot(pair, both, preferred_element_type=F32)
         for j in range(NBK):
             acc[slots[j]] += terms[j * BLOCK : (j + 1) * BLOCK]
-        return carry
-
-    lax.fori_loop(0, H * local, step, 0)
+
+    def step(t, carry):
+        one, two = 2 * t, 2 * t + 1
+        slots_one, both_one, keys_one, mixed_one = begin(one)
+        slots_two, both_two, keys_two, mixed_two = begin(two)
+        pair_one = soften(mixed_one)
+        pair_two = soften(mixed_two)
+        end(one, slots_one, both_one, keys_one, pair_one)
+        end(two, slots_two, both_two, keys_two, pair_two)
+        return carry
+
+    lax.fori_loop(0, H * local // 2, step, 0)
 
     def store(i, carry):
         dkv_ref[i] = acc[i].astype(BF16)
@@ -419,14 +436,14 @@
             for i in range(3) if H == 2 else ():
                 if (k == 0) == (i == 0):
                     lo = (i * S + p) * hc
-                    wout_ref[:, lo : lo + hc] = wo[p, i].astype(F32)
+                    wout_ref[:, lo : lo + hc] = wo[p, i]
     if H == 1:
         for p in range(S):
             both = wo[p, 1].astype(F32)
             three = [wo[p, 0].astype(F32)[:, :HEAD], both[:, :HEAD], both[:, HEAD:]]
             for i in range(3):
                 lo = (i * S + p) * hc
-                wout_ref[:, lo : lo + hc] = three[i]
+                wout_ref[:, lo : lo + hc] = three[i].astype(BF16)
     if H == 2:
         d_copy().wait_send()
     for d in range(1, Z):
@@ -514,7 +531,7 @@
     att, tg, wo = pl.pallas_call(
         functools.partial(reduce_kernel, S, Z, H),
         out_shape=(
-            shape((T, S * hc), BF16), shape((T, D), BF16), shape((W, 3 * S * hc), F32),
+            shape((T, S * hc), BF16), shape((T, D), BF16), shape((W, 3 * S * hc), BF16),
         ),
         in_specs=[VMEM] * 4,
         out_specs=(VMEM,) * 3,
@@ -543,7 +560,7 @@
         ),
         name="reduce",
     )(do.reshape(H, R, LANES), dkv.reshape(Z, R, LANES), tokg, wg)
-    return (att, tg, wo)
+    return (att, tg, wo.astype(F32))
 
 
 def solution(mesh):

time: 150 us -> 139 us (0.927)
  Pallas kernels: 141 us -> 132 us
  local copies, waits for them, and re-layouts: 8.6 us -> 2.78 us
  other arithmetic: 0 us -> 3.49 us
    pallas_call x1, Pallas kernels: 23.7 us -> 15.2 us  [on_device(): pl.pallas_call(functools.partial(attend_kernel, S, Z, H, per_shard), out_...]
    unnamed x4 -> x7, local copies, waits for them, and re-layouts: 8.6 us -> 2.78 us
    convert_element_type x0 -> x1, other arithmetic: none -> 3.49 us  [on_device(): return (att, tg, wo.astype(F32))]
where the time goes in v4:
time: 139 us
  Pallas kernels  132 us (95%)
  other arithmetic  3.49 us (3%)
  local copies, waits for them, and re-layouts  2.78 us (2%)
    pallas_call x1, Pallas kernels, on_device(): pl.pallas_call(functools.partial(reduce_kernel, S, Z, H), out_shape=(shap...  70.3 us
    pallas_call x1, Pallas kernels, on_device(): pl.pallas_call(functools.partial(gather_kernel, S, Z, H), out_shape=(shap...  46.3 us
    pallas_call x1, Pallas kernels, on_device(): pl.pallas_call(functools.partial(attend_kernel, S, Z, H, per_shard), out_...  15.2 us
    convert_element_type x1, other arithmetic, on_device(): return (att, tg, wo.astype(F32))  3.49 us
    unnamed x7, local copies, waits for them, and re-layouts  2.78 us

profile of v4, /device:TPU:11, one launch (start us, length us, event | category | flops | bytes accessed | tf_op | source)
XLA Modules:
  0.0 138.7 jit_solution(439382825901116768)
XLA Ops:
  0.6 1.4 copy.7.pat_ref
  2.0 46.3 %gather.1 = (bf16[1024,1024]{1,0:T(8,128)(2,1)}, bf16[3,1024,128]{2,1,0:T(8,128)(2,1)}, bf16[4,1024,128]{2,1,0:T(8,128)(2,1)}, bf16[2,1024,128]{2,1,0:T(8,128)(2,1)}) custom-call(bf16[128,1024]{1,0:T(8,128)(2,1)} %tok_ref.1, bf16[256,3072]{1,0:T(8,128)(2,1)} %w_ref.1, bf16[128,1024]{1,0:T(8,128)(2,1)} %up_ref.1), custom_call_target="tpu_custom_call" | custom-call | tf_op jit(solution)/shard_map/gather/pallas_call | solution.py:494
  48.3 15.2 %attend.1 = (bf16[16,128,128]{2,1,0:T(8,128)(2,1)}, bf16[32,128,128]{2,1,0:T(8,128)(2,1)}) custom-call(s32[32,8]{1,0:T(8,128)} %copy.7.pat_ref, bf16[16,128,128]{2,1,0:T(8,128)(2,1)} %bitcast.7, bf16[32,128,128]{2,1,0:T(8,128)(2,1)} %bitcast.5), custom_call_target="tpu_custom_call" | custom-call | tf_op jit(solution)/shard_map/attend/pallas_call | solution.py:516
  63.5 70.3 %reduce.1 = (bf16[128,1024]{1,0:T(8,128)(2,1)}, bf16[128,1024]{1,0:T(8,128)(2,1)}, bf16[256,3072]{1,0:T(8,128)(2,1)}) custom-call(bf16[2,1024,128]{2,1,0:T(8,128)(2,1)} %bitcast.6, bf16[4,1024,128]{2,1,0:T(8,128)(2,1)} %bitcast.4, bf16[1024,1024]{1,0:T(8,128)(2,1)} %get-tuple-element.16.tokg_ref, bf16[3,1024,128]{2,1,0:T(8,128)(2,1)} %get-tuple-element.17.wg_ref), custom_call_target="tpu_custom_call" | custom-call | tf_op jit(solution)/shard_map/reduce/pallas_call | solution.py:531
  133.8 0.0 copy-start.1
  133.8 0.0 copy-start
  133.8 3.5 %convert_element_type.3 = f32[256,3072]{1,0:T(8,128)} convert(bf16[256,3072]{1,0:T(8,128)(2,1)} %get-tuple-element.20) | non-fusion elementwise | flops 786432 | bytes 4718592 | tf_op jit(solution)/shard_map/convert_element_type | solution.py:563
  137.3 0.0 copy-done.1
  137.3 0.7 copy.10
  138.0 0.0 copy-done
  138.0 0.7 copy.11
Async XLA Ops:
  133.8 3.5 %copy-start.1 = (bf16[128,1024]{1,0:T(8,128)(2,1)S(1)}, bf16[128,1024]{1,0:T(8,128)(2,1)}, u32[]{:S(2)}) copy-start(bf16[128,1024]{1,0:T(8,128)(2,1)} %get-tuple-element.24) | copy-start | bytes 786436
  133.8 4.2 %copy-start = (bf16[128,1024]{1,0:T(8,128)(2,1)S(1)}, bf16[128,1024]{1,0:T(8,128)(2,1)}, u32[]{:S(2)}) copy-start(bf16[128,1024]{1,0:T(8,128)(2,1)} %get-tuple-element.25) | copy-start | bytes 786436

commit v5 on v4

--- a/solution.py
+++ b/solution.py
@@ -75,8 +75,22 @@
     def w_copy(d, owner, peer):
         return remote(wown, wg_ref.at[:, wrows(owner)], ws.at[d], wr.at[d], (sme, peer))
 
-    def t_copy(d, owner, peer):
-        return remote(tok_ref, tokg_ref.at[rows(owner)], ts.at[d], tr.at[d], (peer, zme))
+    C = S // 2
+    core = lax.rem(sme, 2)
+    chip = sme // 2
+    twin = sme + 1 - 2 * core
+
+    def owner_at(c, side):
+        return lax.rem(chip + C - c, C) * 2 + side
+
+    def t_copy(c, owner):
+        peer = lax.rem(chip + c, C) * 2 + core
+        return remote(tok_ref, tokg_ref.at[rows(owner)], ts.at[c], tr.at[c], (peer, zme))
+
+    def f_copy(c, side):
+        src = tokg_ref.at[rows(owner_at(c, core))]
+        dst = tokg_ref.at[rows(owner_at(c, side))]
+        return remote(src, dst, ts.at[C + c], tr.at[C + c], (twin, zme))
 
     def u_copy(d, owner, peer):
         return remote(up_part(peer), ubuf.at[rows(owner)], us.at[d], ur.at[d], (peer, zme))
@@ -104,12 +118,13 @@
     greet(S, Z, sme, zme)
     for d in range(1, Z):
         w_copy(d, zme, lax.rem(zme + d, Z)).start()
+    tokg_ref[rows(sme), :] = tok_ref[...]
+    for c in range(1, C):
+        t_copy(c, sme).start()
+    f_copy(0, core).start()
     for d in range(1, S):
-        peer = lax.rem(sme + d, S)
-        t_copy(d, sme, peer).start()
-        u_copy(d, sme, peer).start()
+        u_copy(d, sme, lax.rem(sme + d, S)).start()
     wg_ref[:, wrows(zme), :] = wown[...]
-    tokg_ref[rows(sme), :] = tok_ref[...]
     if H == 1:
         ubuf[rows(sme), :] = up_ref[sme]
     else:
@@ -117,8 +132,8 @@
     for d in range(1, Z):
         w_copy(d, lax.rem(zme + Z - d, Z), lax.rem(zme + d, Z)).wait_recv()
 
-    def project(d):
-        block = lax.rem(sme + S - d, S)
+    def project(block):
+        d = lax.rem(sme + S - block, S)
         here = tokg_ref[rows(block), :]
         for h in range(H):
             kvown[h, rows(block), :] = jnp.dot(
@@ -138,16 +153,27 @@
             quown[0, rows(block), :] = jnp.where(half, queries, ubuf[rows(block), :])
         qu_ref[hme, rows(block), :] = quown[hme, rows(block), :]
 
-    project(0)
-
-    def step(d, carry):
-        owner, peer = lax.rem(sme + S - d, S), lax.rem(sme + d, S)
-        t_copy(d, owner, peer).wait_recv()
-        u_copy(d, owner, peer).wait_recv()
-        project(d)
+    def upstream_of(block):
+        d = lax.rem(sme + S - block, S)
+        u_copy(d, block, lax.rem(sme + d, S)).wait_recv()
+
+    project(sme)
+    f_copy(0, 1 - core).wait_recv()
+    upstream_of(twin)
+    project(twin)
+
+    def step(c, carry):
+        same, across = owner_at(c, core), owner_at(c, 1 - core)
+        t_copy(c, same).wait_recv()
+        f_copy(c, core).start()
+        upstream_of(same)
+        project(same)
+        f_copy(c, 1 - core).wait_recv()
+        upstream_of(across)
+        project(across)
         return carry
 
-    lax.fori_loop(1, S, step, 0)
+    lax.fori_loop(1, C, step, 0)
 
     def finish(d, carry):
         block = lax.rem(sme + S - d, S)
@@ -163,9 +189,12 @@
     for d in range(1, S):
         peer = lax.rem(sme + d, S)
         u_copy(d, sme, peer).wait_send()
-        t_copy(d, sme, peer).wait_send()
     for d in range(1, Z):
         w_copy(d, zme, lax.rem(zme + d, Z)).wait_send()
+    for c in range(C):
+        f_copy(c, core).wait_send()
+        if c:
+            t_copy(c, sme).wait_send()
     lax.fori_loop(0, S, finish, 0)
 
 

time: 139 us -> 139 us (level)
  no operation moved by 1% of the time
where the time goes in v5:
time: 139 us
  Pallas kernels  132 us (95%)
  other arithmetic  3.49 us (3%)
  local copies, waits for them, and re-layouts  2.78 us (2%)
    pallas_call x1, Pallas kernels, on_device(): pl.pallas_call(functools.partial(reduce_kernel, S, Z, H), out_shape=(shap...  70 us
    pallas_call x1, Pallas kernels, on_device(): pl.pallas_call(functools.partial(gather_kernel, S, Z, H), out_shape=(shap...  46.8 us
    pallas_call x1, Pallas kernels, on_device(): pl.pallas_call(functools.partial(attend_kernel, S, Z, H, per_shard), out_...  15.2 us
    convert_element_type x1, other arithmetic, on_device(): return (att, tg, wo.astype(F32))  3.49 us
    unnamed x7, local copies, waits for them, and re-layouts  2.78 us

profile of v5, /device:TPU:11, one launch (start us, length us, event | category | flops | bytes accessed | tf_op | source)
XLA Modules:
  0.0 139.0 jit_solution(14196316758908993264)
XLA Ops:
  0.6 1.4 copy.7.pat_ref
  2.0 46.8 %gather.1 = (bf16[1024,1024]{1,0:T(8,128)(2,1)}, bf16[3,1024,128]{2,1,0:T(8,128)(2,1)}, bf16[4,1024,128]{2,1,0:T(8,128)(2,1)}, bf16[2,1024,128]{2,1,0:T(8,128)(2,1)}) custom-call(bf16[128,1024]{1,0:T(8,128)(2,1)} %tok_ref.1, bf16[256,3072]{1,0:T(8,128)(2,1)} %w_ref.1, bf16[128,1024]{1,0:T(8,128)(2,1)} %up_ref.1), custom_call_target="tpu_custom_call" | custom-call | tf_op jit(solution)/shard_map/gather/pallas_call | solution.py:523
  48.8 15.2 %attend.1 = (bf16[16,128,128]{2,1,0:T(8,128)(2,1)}, bf16[32,128,128]{2,1,0:T(8,128)(2,1)}) custom-call(s32[32,8]{1,0:T(8,128)} %copy.7.pat_ref, bf16[16,128,128]{2,1,0:T(8,128)(2,1)} %bitcast.7, bf16[32,128,128]{2,1,0:T(8,128)(2,1)} %bitcast.5), custom_call_target="tpu_custom_call" | custom-call | tf_op jit(solution)/shard_map/attend/pallas_call | solution.py:545
  64.0 70.0 %reduce.1 = (bf16[128,1024]{1,0:T(8,128)(2,1)}, bf16[128,1024]{1,0:T(8,128)(2,1)}, bf16[256,3072]{1,0:T(8,128)(2,1)}) custom-call(bf16[2,1024,128]{2,1,0:T(8,128)(2,1)} %bitcast.6, bf16[4,1024,128]{2,1,0:T(8,128)(2,1)} %bitcast.4, bf16[1024,1024]{1,0:T(8,128)(2,1)} %get-tuple-element.16.tokg_ref, bf16[3,1024,128]{2,1,0:T(8,128)(2,1)} %get-tuple-element.17.wg_ref), custom_call_target="tpu_custom_call" | custom-call | tf_op jit(solution)/shard_map/reduce/pallas_call | solution.py:560
  134.0 0.0 copy-start.1
  134.0 0.0 copy-start
  134.1 3.5 %convert_element_type.3 = f32[256,3072]{1,0:T(8,128)} convert(bf16[256,3072]{1,0:T(8,128)(2,1)} %get-tuple-element.20) | non-fusion elementwise | flops 786432 | bytes 4718592 | tf_op jit(solution)/shard_map/convert_element_type | solution.py:592
  137.5 0.0 copy-done.1
  137.5 0.7 copy.10
  138.3 0.0 copy-done
  138.3 0.7 copy.11
Async XLA Ops:
  134.0 3.5 %copy-start.1 = (bf16[128,1024]{1,0:T(8,128)(2,1)S(1)}, bf16[128,1024]{1,0:T(8,128)(2,1)}, u32[]{:S(2)}) copy-start(bf16[128,1024]{1,0:T(8,128)(2,1)} %get-tuple-element.24) | copy-start | bytes 786436
  134.0 4.2 %copy-start = (bf16[128,1024]{1,0:T(8,128)(2,1)S(1)}, bf16[128,1024]{1,0:T(8,128)(2,1)}, u32[]{:S(2)}) copy-start(bf16[128,1024]{1,0:T(8,128)(2,1)} %get-tuple-element.25) | copy-start | bytes 786436
